TPU v7x, 512 devices: a whole 4x4x16 slice. The times are simulated.
512 devices in a mesh: ctx: 32 (over z_lo, x, core), slab: 16 (over z_hi, y).
Axes of the slice: x: 4, y: 4, z: 16 (z_hi: 4, z_lo: 4; z = z_hi * 4 + z_lo), core: 2. Of those that a mesh axis runs over, the one named last changes fastest.
Arguments:
- query_in: bfloat16 [512, 65536], P('slab', 'ctx'), may hold values from -6 to 6
- key_in: bfloat16 [512, 65536], P('slab', 'ctx'), may hold values from -6 to 6
- value_in: bfloat16 [512, 65536], P('slab', 'ctx'), may hold values from -6 to 6
- grad_out: bfloat16 [512, 65536], P('slab', 'ctx'), may hold values from -6 to 6
- w_first: float32 [33, 64], replicated, may hold values from -1 to 1
- b_first: float32 [64], replicated, may hold values from -3 to 3
- frequency: float32 [64], replicated, may hold values from 2 to 12
- w_second: float32 [64, 512], P(None, 'slab'), may hold values from -0.75 to 0.75
- decay_rate: float32 [512], P('slab'), may hold values from 3.0517579e-06 to 0.03
- skip_gain: float32 [512], P('slab'), may hold values from 0.5 to 1.5
Outputs:
- grad_query: bfloat16 [512, 65536], P('slab', 'ctx')
- grad_key: bfloat16 [512, 65536], P('slab', 'ctx')
- grad_value: bfloat16 [512, 65536], P('slab', 'ctx')
- grad_first: float32 [33, 64], replicated
- grad_bias: float32 [64], replicated
- grad_freq: float32 [64], replicated
- grad_second: float32 [64, 512], P(None, 'slab')
- grad_skip: float32 [512], P('slab')
All inputs are finite; a program needn't handle non-finite values.
Results may differ from a plain program's by a relative error of at most 0.011.
Values may be sent and summed in bfloat16 or wider, within the bound.
A program may use at most 128 MiB of HBM per device.

v0:
```python
import math

import jax
import jax.numpy as jnp
from jax import lax
from jax.sharding import PartitionSpec as P

BANDS = 16


two_pi = 2.0 * math.pi


def features(first_pos, pos_count, seq_len):
    time_ids = first_pos + jnp.arange(pos_count, dtype=jnp.int32)
    freq_ids = jnp.arange(1, BANDS + 1, dtype=jnp.int32)
    phase = (freq_ids[:, None] * time_ids[None, :] % seq_len).astype(jnp.float32) * (
        two_pi / seq_len
    )
    linear = (time_ids.astype(jnp.float32) / seq_len)[None, :]
    return jnp.concatenate([linear, jnp.cos(phase), jnp.sin(phase)], axis=0)


def modulation(decay, first_pos, pos_count, seq_len):
    times = (first_pos + jnp.arange(pos_count, dtype=jnp.int32)).astype(jnp.float32)
    scaling = jnp.sqrt(jnp.expm1(-2.0 * decay) / jnp.expm1(-2.0 * decay * seq_len))
    return jnp.exp(-decay[:, None] * times[None, :]) * scaling[:, None]


def matmul_high(form, left, right):
    return jnp.einsum(form, left, right, precision=lax.Precision.HIGHEST)


def complex_product(left_real, left_imag, right_real, right_imag):
    return (
        left_real * right_real - left_imag * right_imag,
        left_real * right_imag + left_imag * right_real,
    )


def square_table(order_len):
    ids = jnp.arange(order_len, dtype=jnp.int32)
    angle_val = (ids[:, None] * ids[None, :] % order_len).astype(jnp.float32) * (two_pi / order_len)
    return (jnp.cos(angle_val), -jnp.sin(angle_val))


def dft_tables(n_one, n_two):
    cos_one, sin_one = square_table(n_one)
    cos_two, sin_two = square_table(n_two)
    row_ids = jnp.arange(n_one, dtype=jnp.int32)[:, None]
    col_ids = jnp.arange(n_two, dtype=jnp.int32)[None, :]
    angle_val = (row_ids * col_ids % (n_one * n_two)).astype(jnp.float32) * (
        two_pi / (n_one * n_two)
    )
    return (cos_one, sin_one, cos_two, sin_two, jnp.cos(angle_val), -jnp.sin(angle_val))


def forward_dft(signal, tables, n_one, n_two):
    cos_one, sin_one, cos_two, sin_two, twid_cos, twid_sin = tables
    grid = signal.reshape(signal.shape[0], n_one, n_two)
    a_real = matmul_high("bnm,nk->bkm", grid, cos_one)
    a_imag = matmul_high("bnm,nk->bkm", grid, sin_one)
    b_real, b_imag = complex_product(a_real, a_imag, twid_cos, twid_sin)
    out_real = matmul_high("bkm,mj->bkj", b_real, cos_two) - matmul_high(
        "bkm,mj->bkj", b_imag, sin_two
    )
    out_imag = matmul_high("bkm,mj->bkj", b_real, sin_two) + matmul_high(
        "bkm,mj->bkj", b_imag, cos_two
    )
    return (out_real, out_imag)


def inverse_dft(spec_real, spec_imag, tables, n_one, n_two):
    cos_one, sin_one, cos_two, sin_two, twid_cos, twid_sin = tables
    c_real = matmul_high("bkj,jm->bkm", spec_real, cos_two) + matmul_high(
        "bkj,jm->bkm", spec_imag, sin_two
    )
    c_imag = matmul_high("bkj,jm->bkm", spec_imag, cos_two) - matmul_high(
        "bkj,jm->bkm", spec_real, sin_two
    )
    d_real = c_real * twid_cos + c_imag * twid_sin
    d_imag = c_imag * twid_cos - c_real * twid_sin
    result = matmul_high("bkm,kn->bnm", d_real, cos_one) + matmul_high(
        "bkm,kn->bnm", d_imag, sin_one
    )
    return result.reshape(result.shape[0], n_one * n_two) / (n_one * n_two)


def spectral(filter_vals, mixed_c, grads_c):
    chan_each, seq_len = filter_vals.shape
    padded_len = 2 * seq_len
    bit_count = padded_len.bit_length() - 1
    n_one = 2 ** (bit_count // 2)
    n_two = padded_len // n_one
    tables = dft_tables(n_one, n_two)
    stacked = jnp.concatenate(
        [filter_vals, mixed_c.astype(jnp.float32), grads_c.astype(jnp.float32)], axis=0
    )
    stacked = jnp.pad(stacked, ((0, 0), (0, seq_len)))
    spec_real, spec_imag = forward_dft(stacked, tables, n_one, n_two)
    h_real, w_real, g_real = (
        spec_real[:chan_each],
        spec_real[chan_each : 2 * chan_each],
        spec_real[2 * chan_each :],
    )
    h_imag, w_imag, g_imag = (
        spec_imag[:chan_each],
        spec_imag[chan_each : 2 * chan_each],
        spec_imag[2 * chan_each :],
    )
    conv_real, conv_imag = complex_product(h_real, h_imag, w_real, w_imag)
    back_real, back_imag = complex_product(h_real, -h_imag, g_real, g_imag)
    grad_real, grad_imag = complex_product(w_real, -w_imag, g_real, g_imag)
    all_real = jnp.concatenate([conv_real, back_real, grad_real], axis=0)
    all_imag = jnp.concatenate([conv_imag, back_imag, grad_imag], axis=0)
    signals = inverse_dft(all_real, all_imag, tables, n_one, n_two)[:, :seq_len]
    return (signals[:chan_each], signals[chan_each : 2 * chan_each], signals[2 * chan_each :])


def shards(
    query_in,
    key_in,
    value_in,
    grad_out,
    w_first,
    b_first,
    frequency,
    w_second,
    decay_rate,
    skip_gain,
):
    high = lax.Precision.HIGHEST
    ctx_count = lax.axis_size("ctx")
    chan_count, seq_part = query_in.shape
    seq_len = seq_part * ctx_count
    chan_each = chan_count // ctx_count
    ctx_index = lax.axis_index("ctx")
    chan_start = ctx_index * chan_each
    mixed = (key_in.astype(jnp.float32) * value_in.astype(jnp.float32)).astype(jnp.bfloat16)
    grad_mid = (grad_out.astype(jnp.float32) * query_in.astype(jnp.float32)).astype(jnp.bfloat16)
    mixed_c, grads_c = (
        lax.all_to_all(mixed, "ctx", split_axis=0, concat_axis=1, tiled=True),
        lax.all_to_all(grad_mid, "ctx", split_axis=0, concat_axis=1, tiled=True),
    )
    my_skip = lax.dynamic_slice_in_dim(skip_gain, chan_start, chan_each)
    feature_rows = features(ctx_index * seq_part, seq_part, seq_len)
    pre_act = jnp.dot(w_first.T, feature_rows, precision=high) + b_first[:, None]
    hidden = jnp.sin(frequency[:, None] * pre_act)
    mod_used = modulation(decay_rate, ctx_index * seq_part, seq_part, seq_len)
    filter_local = jnp.dot(w_second.T, hidden, precision=high) * mod_used
    filter_vals = lax.all_to_all(filter_local, "ctx", split_axis=0, concat_axis=1, tiled=True)
    conv_out, back_raw, grad_filter = spectral(filter_vals, mixed_c, grads_c)
    middle_c = (conv_out + my_skip[:, None] * mixed_c.astype(jnp.float32)).astype(jnp.bfloat16)
    back_c = (back_raw + my_skip[:, None] * grads_c.astype(jnp.float32)).astype(jnp.bfloat16)
    middle, back_out = (
        lax.all_to_all(middle_c, "ctx", split_axis=1, concat_axis=0, tiled=True),
        lax.all_to_all(back_c, "ctx", split_axis=1, concat_axis=0, tiled=True),
    )
    grad_query = (grad_out.astype(jnp.float32) * middle.astype(jnp.float32)).astype(jnp.bfloat16)
    grad_key = (back_out.astype(jnp.float32) * value_in.astype(jnp.float32)).astype(jnp.bfloat16)
    grad_value = (back_out.astype(jnp.float32) * key_in.astype(jnp.float32)).astype(jnp.bfloat16)
    skip_part = jnp.sum(grad_mid.astype(jnp.float32) * mixed.astype(jnp.float32), axis=1)
    filter_seq = lax.all_to_all(
        grad_filter.astype(jnp.bfloat16), "ctx", split_axis=1, concat_axis=0, tiled=True
    ).astype(grad_filter.dtype)
    grad_mod = filter_seq * mod_used
    second_part = jnp.dot(hidden, grad_mod.T, precision=high)
    grad_second, grad_skip = lax.psum((second_part, skip_part), "ctx")
    grad_hidden = jnp.dot(w_second, grad_mod, precision=high)
    grad_sin = grad_hidden * jnp.cos(frequency[:, None] * pre_act)
    freq_part = jnp.sum(grad_sin * pre_act, axis=1)
    grad_pre = grad_sin * frequency[:, None]
    bias_part = jnp.sum(grad_pre, axis=1)
    first_part = jnp.dot(feature_rows, grad_pre.T, precision=high)
    grad_first, grad_bias, grad_freq = lax.psum((first_part, bias_part, freq_part), ("ctx", "slab"))
    return (
        grad_query,
        grad_key,
        grad_value,
        grad_first,
        grad_bias,
        grad_freq,
        grad_second,
        grad_skip,
    )


def solution(mesh):
    placed = (
        P("slab", "ctx"),
        P("slab", "ctx"),
        P("slab", "ctx"),
        P("slab", "ctx"),
        P(),
        P(),
        P(),
        P(None, "slab"),
        P("slab"),
        P("slab"),
    )
    return jax.shard_map(
        shards,
        mesh=mesh,
        in_specs=placed,
        out_specs=(
            P("slab", "ctx"),
            P("slab", "ctx"),
            P("slab", "ctx"),
            P(),
            P(),
            P(),
            P(None, "slab"),
            P("slab"),
        ),
        check_vma=False,
    )
```

profile of v0, /device:TPU:1, one launch (start us, length us, event | category | flops | bytes accessed | tf_op | source)
XLA Modules:
  0.0 406.7 jit_solution(9758573033747117302)
XLA Ops:
  0.7 1.3 multiply_reduce_fusion.2
  2.5 0.7 reduce
  3.2 0.7 reshape.184
  3.9 10.4 %all-to-all-start.2 = ((bf16[32,2,1024]{2,1,0:T(2,128)(2,1)}), bf16[32,2,1024]{2,1,0:T(2,128)(2,1)S(1)}, u32[]{:S(2)}, u32[]{:S(2)}) async-start(bf16[32,2,1024]{2,1,0:T(2,128)(2,1)} %reshape.184), calls=%async_computation.2 | async-start | bytes 262144 | tf_op jit(solution)/shard_map/all_to_all | solution.py:143
  14.4 0.7 reduce.1
  15.1 0.7 reshape.186
  16.4 6.6 %all-to-all-done.2 = bf16[32,2,1024]{2,1,0:T(2,128)(2,1)S(1)} async-done(((bf16[32,2,1024]{2,1,0:T(2,128)(2,1)}), bf16[32,2,1024]{2,1,0:T(2,128)(2,1)S(1)}, u32[]{:S(2)}, u32[]{:S(2)}) %all-to-all-start.2) | async-done | bytes 131104 | tf_op jit(solution)/shard_map/all_to_all | solution.py:143
  23.0 3.9 all-to-all-start.1
  27.6 2.2 fusion.3
  29.8 1.0 copy.23
  30.7 4.8 %all-to-all-done.1 = bf16[32,2,1024]{2,1,0:T(2,128)(2,1)S(1)} async-done(((bf16[32,2,1024]{2,1,0:T(2,128)(2,1)}), bf16[32,2,1024]{2,1,0:T(2,128)(2,1)S(1)}, u32[]{:S(2)}, u32[]{:S(2)}) %all-to-all-start.1) | async-done | bytes 131104 | tf_op jit(solution)/shard_map/all_to_all | solution.py:142
  35.6 4.1 %all-to-all-start = ((f32[32,1,2048]{2,1,0:T(1,128)}), f32[32,1,2048]{2,1,0:T(1,128)S(1)}, u32[]{:S(2)}, u32[]{:S(2)}) async-start(f32[32,1,2048]{2,1,0:T(1,128)} %copy.23), calls=%async_computation | async-start | bytes 524288 | tf_op jit(solution)/shard_map/all_to_all | solution.py:151
  40.2 2.1 sine_negate_fusion.5
  43.1 7.6 %all-to-all-done = f32[32,1,2048]{2,1,0:T(1,128)S(1)} async-done(((f32[32,1,2048]{2,1,0:T(1,128)}), f32[32,1,2048]{2,1,0:T(1,128)S(1)}, u32[]{:S(2)}, u32[]{:S(2)}) %all-to-all-start) | async-done | bytes 262176 | tf_op jit(solution)/shard_map/all_to_all | solution.py:151
  50.7 0.8 select_maximum_fusion
  51.5 2.8 fusion.4
  54.3 2.7 fusion.6
  57.0 6.9 %fusion.8 = f32[3,256,512]{2,1,0:T(8,128)S(1)} fusion(f32[256,3,512]{2,0,1:T(8,128)S(1)} %fusion.4, f32[256,3,512]{2,0,1:T(8,128)S(1)} %fusion.6, f32[256,512]{1,0:T(8,128)S(1)} %get-tuple-element.35, f32[256,512]{1,0:T(8,128)S(1)} %get-tuple-element.36), kind=kOutput, calls=%fused_computation.16 | convolution fusion | flops 2420768768 | bytes 5767168 | tf_op jit(solution)/shard_map/bkm,mj->bkj/dot_general | solution.py:31
  63.9 6.7 %fusion.10 = f32[3,256,512]{2,1,0:T(8,128)S(1)} fusion(f32[256,3,512]{2,0,1:T(8,128)S(1)} %fusion.4, f32[256,3,512]{2,0,1:T(8,128)S(1)} %fusion.6, f32[256,512]{1,0:T(8,128)S(1)} %get-tuple-element.35, f32[256,512]{1,0:T(8,128)S(1)} %get-tuple-element.36), kind=kOutput, calls=%fused_computation.18 | convolution fusion | flops 2421030912 | bytes 5767168 | tf_op jit(solution)/shard_map/bkm,mj->bkj/dot_general | solution.py:31
  70.6 7.1 %fusion.29 = f32[3,256,512]{2,1,0:T(8,128)S(1)} fusion(f32[3,256,512]{2,1,0:T(8,128)S(1)} %fusion.8, f32[256,3,512]{2,0,1:T(8,128)S(1)} %fusion.4, f32[256,3,512]{2,0,1:T(8,128)S(1)} %fusion.6, f32[256,512]{1,0:T(8,128)S(1)} %get-tuple-element.35, f32[256,512]{1,0:T(8,128)S(1)} %get-tuple-element.36), kind=kOutput, calls=%fused_computation.39 | convolution fusion | flops 2421424128 | bytes 7340032 | tf_op jit(solution)/shard_map/bkm,mj->bkj/dot_general | solution.py:31
  77.7 6.6 %fusion.26 = f32[3,256,512]{2,1,0:T(8,128)S(1)} fusion(f32[3,256,512]{2,1,0:T(8,128)S(1)} %fusion.10, f32[256,3,512]{2,0,1:T(8,128)S(1)} %fusion.4, f32[256,3,512]{2,0,1:T(8,128)S(1)} %fusion.6, f32[256,512]{1,0:T(8,128)S(1)} %get-tuple-element.35, f32[256,512]{1,0:T(8,128)S(1)} %get-tuple-element.36), kind=kOutput, calls=%fused_computation.38 | convolution fusion | flops 2421161984 | bytes 7340032 | tf_op jit(solution)/shard_map/bkm,mj->bkj/dot_general | solution.py:31
  85.3 6.5 %fusion.35 = f32[3,256,512]{2,1,0:T(8,128)S(1)} fusion(f32[1,256,512]{2,1,0:T(8,128)S(1)} %get-tuple-element.16, f32[1,256,512]{2,1,0:T(8,128)S(1)} %get-tuple-element.20, f32[1,256,512]{2,1,0:T(8,128)S(1)} %get-tuple-element.19), kind=kOutput, calls=%fused_computation.45 | convolution fusion | flops 2420375552 | bytes 3145728 | tf_op jit(solution)/shard_map/bkj,jm->bkm/dot_general | solution.py:31
  91.8 6.7 %fusion.34 = f32[3,256,512]{2,1,0:T(8,128)S(1)} fusion(f32[1,256,512]{2,1,0:T(8,128)S(1)} %get-tuple-element.18, f32[1,256,512]{2,1,0:T(8,128)S(1)} %get-tuple-element.17, f32[1,256,512]{2,1,0:T(8,128)S(1)} %get-tuple-element.15), kind=kOutput, calls=%fused_computation.44 | convolution fusion | flops 2420375552 | bytes 3145728 | tf_op jit(solution)/shard_map/bkj,jm->bkm/dot_general | solution.py:31
  98.5 6.6 %convolution_add_fusion.1 = f32[3,256,512]{2,1,0:T(8,128)S(1)} fusion(f32[3,256,512]{2,1,0:T(8,128)S(1)} %fusion.35, f32[1,256,512]{2,1,0:T(8,128)S(1)} %get-tuple-element.18, f32[1,256,512]{2,1,0:T(8,128)S(1)} %get-tuple-element.17, f32[1,256,512]{2,1,0:T(8,128)S(1)} %get-tuple-element.15), kind=kOutput, calls=%fused_computation.41 | convolution fusion | flops 2421030912 | bytes 4718592 | tf_op jit(solution)/shard_map/bkj,jm->bkm/dot_general | solution.py:31
  105.1 6.9 %convolution_subtract_fusion = f32[3,256,512]{2,1,0:T(8,128)S(1)} fusion(f32[3,256,512]{2,1,0:T(8,128)S(1)} %fusion.34, f32[1,256,512]{2,1,0:T(8,128)S(1)} %get-tuple-element.16, f32[1,256,512]{2,1,0:T(8,128)S(1)} %get-tuple-element.20, f32[1,256,512]{2,1,0:T(8,128)S(1)} %get-tuple-element.19), kind=kOutput, calls=%fused_computation.40 | convolution fusion | flops 2421030912 | bytes 4718592 | tf_op jit(solution)/shard_map/bkj,jm->bkm/dot_general | solution.py:31
  112.1 2.7 fusion.16
  114.8 2.7 multiply_bitcast_fusion
  117.5 1.1 copy.30
  118.6 1.0 slice.81
  119.6 3.0 reduce.4
  122.5 1.6 reshape.192
  124.2 4.8 %all-to-all-start.5 = ((bf16[32,2,1024]{2,1,0:T(2,128)(2,1)}), bf16[32,2,1024]{2,1,0:T(2,128)(2,1)}, u32[]{:S(2)}, u32[]{:S(2)}) async-start(bf16[32,2,1024]{2,1,0:T(2,128)(2,1)} %reshape.192), calls=%async_computation.5 | async-start | bytes 262144 | tf_op jit(solution)/shard_map/all_to_all | solution.py:163
  128.9 2.1 fusion.80
  131.1 2.3 reduce.3
  133.4 0.7 reshape.190
  134.1 3.3 all-to-all-done.5
  137.5 4.5 %all-to-all-start.4 = ((bf16[32,2,1024]{2,1,0:T(2,128)(2,1)}), bf16[32,2,1024]{2,1,0:T(2,128)(2,1)S(1)}, u32[]{:S(2)}, u32[]{:S(2)}) async-start(bf16[32,2,1024]{2,1,0:T(2,128)(2,1)} %reshape.190), calls=%async_computation.4 | async-start | bytes 262144 | tf_op jit(solution)/shard_map/all_to_all | solution.py:157
  142.0 2.3 reduce.2
  144.3 0.7 reshape.188
  145.0 1.4 reshape.193
  146.4 2.4 fusion.71
  148.8 2.5 multiply_reduce_fusion
  151.3 7.9 %all-to-all-start.3 = ((bf16[32,2,1024]{2,1,0:T(2,128)(2,1)}), bf16[32,2,1024]{2,1,0:T(2,128)(2,1)S(1)}, u32[]{:S(2)}, u32[]{:S(2)}) async-start(bf16[32,2,1024]{2,1,0:T(2,128)(2,1)} %reshape.188), calls=%async_computation.3 | async-start | bytes 262144 | tf_op jit(solution)/shard_map/all_to_all | solution.py:156
  159.9 0.8 fusion.76
  160.7 7.0 %all-to-all-done.3 = bf16[32,2,1024]{2,1,0:T(2,128)(2,1)S(1)} async-done(((bf16[32,2,1024]{2,1,0:T(2,128)(2,1)}), bf16[32,2,1024]{2,1,0:T(2,128)(2,1)S(1)}, u32[]{:S(2)}, u32[]{:S(2)}) %all-to-all-start.3) | async-done | bytes 131104 | tf_op jit(solution)/shard_map/all_to_all | solution.py:156
  167.8 0.7 fusion.73
  168.5 129.0 %all-reduce.2 = (f32[64,32]{0,1:T(8,128)}, f32[32]{0:T(128)}) all-reduce(f32[64,32]{0,1:T(8,128)S(1)} %fusion.71, f32[32]{0:T(128)S(1)} %get-tuple-element.23), channel_id=1, replica_groups=mesh['ctx'=32,'slab'=16] {'ctx'}, use_global_device_ids=true, to_apply=%region_5.6 | all-reduce | flops 2080 | bytes 16640 | tf_op jit(solution)/shard_map/psum | solution.py:168
  297.6 108.9 %all-reduce.1 = (f32[33,64]{1,0:T(8,128)}, f32[64]{0:T(128)}, f32[64]{0:T(128)}) all-reduce(f32[33,64]{1,0:T(8,128)S(1)} %fusion.69, f32[64]{0:T(128)S(1)} %get-tuple-element.9, f32[64]{0:T(128)S(1)} %get-tuple-element.8), channel_id=1, replica_groups=mesh['ctx'=32,'slab'=16] {'ctx','slab'}, use_global_device_ids=true, to_apply=%region_0.1 | all-reduce | flops 2240 | bytes 17920 | tf_op jit(solution)/shard_map/psum | solution.py:175
  (36 shorter events, 4.9 us)
Async XLA Ops:
  0.6 26.3 %copy-start = (f32[33,64]{1,0:T(8,128)S(1)}, f32[33,64]{1,0:T(8,128)}, u32[]{:S(2)}) copy-start(f32[33,64]{1,0:T(8,128)} %param.14) | copy-start | bytes 25348
  0.7 26.2 %copy-start.7 = (f32[32]{0:T(128)S(1)}, f32[32]{0:T(128)}, u32[]{:S(2)}) copy-start(f32[32]{0:T(128)} %param.18) | copy-start | bytes 388
  0.7 26.3 %copy-start.6 = (f32[64]{0:T(128)S(1)}, f32[64]{0:T(128)}, u32[]{:S(2)}) copy-start(f32[64]{0:T(128)} %param.15) | copy-start | bytes 772
  0.7 26.9 %copy-start.5 = (f32[64]{0:T(128)S(1)}, f32[64]{0:T(128)}, u32[]{:S(2)}) copy-start(f32[64]{0:T(128)} %param.16) | copy-start | bytes 772
  0.7 26.9 %copy-start.4 = (f32[64,32]{0,1:T(8,128)S(1)}, f32[64,32]{0,1:T(8,128)}, u32[]{:S(2)}) copy-start(f32[64,32]{0,1:T(8,128)} %param.17) | copy-start | bytes 24580
  3.9 19.1 %all-to-all-start.2 = ((bf16[32,2,1024]{2,1,0:T(2,128)(2,1)}), bf16[32,2,1024]{2,1,0:T(2,128)(2,1)S(1)}, u32[]{:S(2)}, u32[]{:S(2)}) async-start(bf16[32,2,1024]{2,1,0:T(2,128)(2,1)} %reshape.184), calls=%async_computation.2 | async-start | bytes 262144 | tf_op jit(solution)/shard_map/all_to_all | solution.py:143
  15.8 23.8 %copy-start.8 = (f32[32]{0:T(128)S(1)}, f32[32]{0:T(128)}, u32[]{:S(2)}) copy-start(f32[32]{0:T(128)} %param.19) | copy-start | bytes 388
  23.0 12.6 %all-to-all-start.1 = ((bf16[32,2,1024]{2,1,0:T(2,128)(2,1)}), bf16[32,2,1024]{2,1,0:T(2,128)(2,1)S(1)}, u32[]{:S(2)}, u32[]{:S(2)}) async-start(bf16[32,2,1024]{2,1,0:T(2,128)(2,1)} %reshape.186), calls=%async_computation.1 | async-start | bytes 262144 | tf_op jit(solution)/shard_map/all_to_all | solution.py:142
  35.6 15.1 %all-to-all-start = ((f32[32,1,2048]{2,1,0:T(1,128)}), f32[32,1,2048]{2,1,0:T(1,128)S(1)}, u32[]{:S(2)}, u32[]{:S(2)}) async-start(f32[32,1,2048]{2,1,0:T(1,128)} %copy.23), calls=%async_computation | async-start | bytes 524288 | tf_op jit(solution)/shard_map/all_to_all | solution.py:151
  124.2 13.3 %all-to-all-start.5 = ((bf16[32,2,1024]{2,1,0:T(2,128)(2,1)}), bf16[32,2,1024]{2,1,0:T(2,128)(2,1)}, u32[]{:S(2)}, u32[]{:S(2)}) async-start(bf16[32,2,1024]{2,1,0:T(2,128)(2,1)} %reshape.192), calls=%async_computation.5 | async-start | bytes 262144 | tf_op jit(solution)/shard_map/all_to_all | solution.py:163
  137.5 13.8 %all-to-all-start.4 = ((bf16[32,2,1024]{2,1,0:T(2,128)(2,1)}), bf16[32,2,1024]{2,1,0:T(2,128)(2,1)S(1)}, u32[]{:S(2)}, u32[]{:S(2)}) async-start(bf16[32,2,1024]{2,1,0:T(2,128)(2,1)} %reshape.190), calls=%async_computation.4 | async-start | bytes 262144 | tf_op jit(solution)/shard_map/all_to_all | solution.py:157
  148.8 11.1 %copy-start.1 = (bf16[32,2048]{1,0:T(8,128)(2,1)S(1)}, bf16[32,2048]{1,0:T(8,128)(2,1)}, u32[]{:S(2)}) copy-start(bf16[32,2048]{1,0:T(8,128)(2,1)} %param.12) | copy-start | bytes 393220
  148.8 11.1 %copy-start.2 = (bf16[32,2048]{1,0:T(8,128)(2,1)S(1)}, bf16[32,2048]{1,0:T(8,128)(2,1)}, u32[]{:S(2)}) copy-start(bf16[32,2048]{1,0:T(8,128)(2,1)} %param.11) | copy-start | bytes 393220
  151.2 16.6 %copy-start.3 = (bf16[32,2048]{1,0:T(8,128)(2,1)S(1)}, bf16[32,2048]{1,0:T(8,128)(2,1)}, u32[]{:S(2)}) copy-start(bf16[32,2048]{1,0:T(8,128)(2,1)} %param.13) | copy-start | bytes 393220
  151.3 16.4 %all-to-all-start.3 = ((bf16[32,2,1024]{2,1,0:T(2,128)(2,1)}), bf16[32,2,1024]{2,1,0:T(2,128)(2,1)S(1)}, u32[]{:S(2)}, u32[]{:S(2)}) async-start(bf16[32,2,1024]{2,1,0:T(2,128)(2,1)} %reshape.188), calls=%async_computation.3 | async-start | bytes 262144 | tf_op jit(solution)/shard_map/all_to_all | solution.py:156
where the time goes:
time: 412 us; the launch traced here: 407 us
  blocking collectives  238 us (58%)
  matrix products  73.2 us (18%)
  starting transfers between devices  35.5 us (9%)
  waiting for transfers between devices  29.3 us (7%)
  other arithmetic  18.9 us (5%)
  local copies, waits for them, and re-layouts  10.5 us (3%)
    psum x1, blocking collectives, shards(): grad_second, grad_skip = lax.psum((second_part, skip_part), 'ctx')  129 us
    psum x1, blocking collectives, shards(): lax.psum((first_part, bias_part, freq_part), ('ctx', 'slab'))  109 us
    dot_general x12, matrix products, matmul_high(): return jnp.einsum(form, left, right, precision=lax.Precision.HIGHEST)  64.9 us
    all_to_all x1, starting transfers between devices, shards(): lax.all_to_all(grad_mid, 'ctx', split_axis=0, concat_axis=1, tiled=True)  10.4 us
  transfers between devices with their start and end apart: 6, of which 5 were waited for; matrix products, arithmetic and copies ran while one was open for 6% of the time, Pallas kernels for 0%

commit v1 on v0

v1 whole, which is shorter than its diff:
```python
import math

import jax
import jax.numpy as jnp
import ml_dtypes
import numpy as np
from jax import lax
from jax.experimental import pallas as pl
from jax.experimental.pallas import tpu as pltpu
from jax.sharding import PartitionSpec as P

BANDS = 16
CTX = 32
SLAB = 16
CHAN = 32
PART = 2048
SEQ = CTX * PART
ROWS = 16
LANES = 128
N_ONE = SEQ // LANES
ORDER = 64
KROWS = 40
PIECE = 4

MESH = pl.DeviceIdType.MESH
f32, bf16 = jnp.float32, jnp.bfloat16


def np_parts(table, count):
    out, rest = [], np.asarray(table, np.float64)
    for _ in range(count):
        part = rest.astype(np.float32).astype(ml_dtypes.bfloat16)
        out.append(part)
        rest = rest - part.astype(np.float64)
    return out


def tables():
    k_one = np.arange(N_ONE)[:, None]
    n_one = np.arange(N_ONE)[None, :]
    phase = 2 * np.pi * (((4 * k_one + 1) * n_one) % (4 * N_ONE)) / (4 * N_ONE)
    first = np.concatenate([np.cos(phase), -np.sin(phase)], axis=0)
    n_two = np.arange(LANES)[None, :]
    turn = 2 * np.pi * (k_one + 0.25) * n_two / SEQ
    twiddle = np.concatenate([np.cos(turn), np.sin(turn)], axis=1).astype(np.float32)
    small = 2 * np.pi * ((np.arange(LANES)[:, None] * n_two) % LANES) / LANES
    cos_s, sin_s = np.cos(small), np.sin(small)
    second = np.block([[cos_s, -sin_s], [sin_s, cos_s]])
    second_inv = np.block([[cos_s, sin_s], [-sin_s, cos_s]])
    place = np.arange(PART)
    bands = np.arange(1, BANDS + 1)
    arc = 2 * np.pi * (bands[:, None] * place[None, :] % SEQ) / SEQ
    base = np.zeros((KROWS, PART))
    base[:BANDS], base[BANDS : 2 * BANDS] = np.cos(arc), np.sin(arc)
    base[2 * BANDS], base[2 * BANDS + 1] = place / SEQ, 1.0
    b_one, b_two, b_three = np_parts(base, 3)
    stacked = np.concatenate([b_one, b_two, b_one, b_three, b_two, b_one], axis=0)
    pair = np.zeros((96, PART), ml_dtypes.bfloat16)
    pair[:KROWS], pair[48 : 48 + KROWS] = b_one, b_two
    start = 2 * np.pi * (bands[None, :] * np.arange(CTX)[:, None] % CTX) / CTX
    rot = np.stack([np.cos(start), np.sin(start)], axis=1).astype(np.float32)
    rot = np.broadcast_to(rot[:, :, :, None], (CTX, 2, BANDS, LANES)).copy()
    one = lambda table: np_parts(table, 1)[0]
    return (
        one(first),
        one(first.T / SEQ),
        one(second),
        one(second_inv),
        twiddle,
        stacked,
        pair,
        rot,
    )


def dot(left, right):
    return jnp.dot(left, right, preferred_element_type=f32)


def dot_first(left, right):
    return lax.dot_general(left, right, (((0,), (0,)), ((), ())), preferred_element_type=f32)


def dot_last(left, right):
    return lax.dot_general(left, right, (((1,), (1,)), ((), ())), preferred_element_type=f32)


def high_low(value):
    high = value.astype(bf16)
    return high, (value - high.astype(f32)).astype(bf16)


def eye(count):
    rows = lax.broadcasted_iota(jnp.int32, (count, count), 0)
    return rows == lax.broadcasted_iota(jnp.int32, (count, count), 1)


def as_column(row, count):
    spread = jnp.broadcast_to(row, (count, count))
    return jnp.sum(jnp.where(eye(count), spread, 0.0), axis=1, keepdims=True)


def as_row(column, count):
    spread = jnp.broadcast_to(column, (count, count))
    return jnp.sum(jnp.where(eye(count), spread, 0.0), axis=0, keepdims=True)


def sine_cosine(quarters):
    whole = jnp.floor(quarters + 0.5)
    rest = quarters - whole
    turn = whole.astype(jnp.int32)
    angle = rest * (math.pi / 2)
    square = angle * angle
    sine = angle + angle * square * (
        -1.0 / 6 + square * (1.0 / 120 + square * (-1.0 / 5040 + square * (1.0 / 362880)))
    )
    cosine = 1.0 + square * (
        -0.5 + square * (1.0 / 24 + square * (-1.0 / 720 + square * (1.0 / 40320)))
    )
    swap = (turn & 1) == 1
    sin_val = jnp.where(swap, cosine, sine)
    cos_val = jnp.where(swap, sine, cosine)
    sin_val = jnp.where((turn & 2) == 2, -sin_val, sin_val)
    cos_val = jnp.where(((turn + 1) & 2) == 2, -cos_val, cos_val)
    return sin_val, cos_val


def main_kernel(
    query_ref,
    key_ref,
    value_ref,
    grad_ref,
    w_first_ref,
    b_first_ref,
    freq_ref,
    w_second_ref,
    decay_ref,
    skip_ref,
    first_hbm,
    first_t_hbm,
    second_hbm,
    second_inv_hbm,
    twiddle_hbm,
    stacked_hbm,
    pair_hbm,
    rot_hbm,
    mid_out,
    back_out,
    sums_out,
    first,
    first_t,
    second,
    second_inv,
    twiddle,
    stacked,
    pair,
    rot,
    flat_a,
    flat_b,
    send_mg,
    recv_mg,
    send_f,
    recv_f,
    send_gf,
    recv_gf,
    send_mb,
    recv_mb,
    weights,
    weight_stack,
    quarters,
    hidden,
    cosines,
    modul,
    both,
    spec_w,
    spec_g,
    fold_a,
    fold_b,
    grad_mod,
    grad_sin,
    pay,
    send_p,
    recv_p,
    piece,
    recv_s,
    done,
    recv_d,
    table_sem,
    send_sem,
    recv_sem,
):
    me = lax.axis_index("ctx")
    slab = lax.axis_index("slab")

    barrier = pltpu.get_barrier_semaphore()

    def greet_ctx(step, carry):
        pl.semaphore_signal(
            barrier, inc=1, device_id={"ctx": lax.rem(me + step, CTX)}, device_id_type=MESH
        )
        return carry

    def greet_slab(step, carry):
        pl.semaphore_signal(
            barrier, inc=1, device_id={"slab": lax.rem(slab + step, SLAB)}, device_id_type=MESH
        )
        return carry

    lax.fori_loop(1, CTX, greet_ctx, 0)
    lax.fori_loop(1, SLAB, greet_slab, 0)

    loads = [
        pltpu.make_async_copy(source, target, table_sem.at[at])
        for at, (source, target) in enumerate(
            [
                (rot_hbm.at[me], rot),
                (stacked_hbm, stacked),
                (first_hbm, first),
                (second_hbm, second),
                (second_inv_hbm, second_inv),
                (twiddle_hbm, twiddle),
                (first_t_hbm, first_t),
                (pair_hbm, pair),
            ]
        )
    ]
    for load in loads:
        load.start()

    def send_all(source, target, at):
        def body(step, carry):
            peer = lax.rem(me + step, CTX)
            pltpu.make_async_remote_copy(
                src_ref=source.at[peer],
                dst_ref=target.at[me],
                send_sem=send_sem.at[at],
                recv_sem=recv_sem.at[at],
                device_id={"ctx": peer},
                device_id_type=MESH,
            ).start()
            return carry

        lax.fori_loop(1, CTX, body, 0)
        pltpu.make_async_copy(source.at[me], target.at[me], recv_sem.at[at]).start()

    def wait_all(target, at):
        pltpu.make_async_copy(target, target, recv_sem.at[at]).wait()

    def wait_sent(source, count, at):
        part = source.at[pl.ds(0, count)]
        pltpu.make_async_copy(part, part, send_sem.at[at]).wait()

    skip_acc = jnp.zeros((CHAN, LANES), f32)
    for col in range(ROWS):
        lanes = pl.ds(col * LANES, LANES)
        mixed = key_ref[:, lanes].astype(f32) * value_ref[:, lanes].astype(f32)
        mixed = mixed.astype(bf16).astype(f32)
        mid = grad_ref[:, lanes].astype(f32) * query_ref[:, lanes].astype(f32)
        mid = mid.astype(bf16).astype(f32)
        flat_a[pl.ds(col, CHAN, stride=ROWS), :] = mixed
        flat_b[pl.ds(col, CHAN, stride=ROWS), :] = mid
        skip_acc = skip_acc + mixed * mid
    send_mg[:, 0] = flat_a[...].reshape(CHAN, ROWS, LANES).astype(bf16)
    send_mg[:, 1] = flat_b[...].reshape(CHAN, ROWS, LANES).astype(bf16)
    skip_row = as_row(jnp.sum(skip_acc, axis=1, keepdims=True), CHAN)

    pl.semaphore_wait(barrier, CTX + SLAB - 2)
    send_all(send_mg, recv_mg, 0)

    loads[0].wait()
    cos_at, sin_at = rot[0][:, :ORDER], rot[1][:, :ORDER]
    w_lin = w_first_ref[0:1, :]
    w_cos = w_first_ref[1 : 1 + BANDS, :]
    w_sin = w_first_ref[1 + BANDS : 1 + 2 * BANDS, :]
    start_frac = me.astype(f32) * (1.0 / CTX)
    weights[...] = jnp.zeros((KROWS, ORDER), f32)
    weights[0:BANDS, :] = w_cos * cos_at + w_sin * sin_at
    weights[BANDS : 2 * BANDS, :] = w_sin * cos_at - w_cos * sin_at
    weights[2 * BANDS : 2 * BANDS + 1, :] = w_lin
    freq_row = freq_ref[...].reshape(1, ORDER)
    weights[2 * BANDS + 1 : 2 * BANDS + 2, :] = (
        b_first_ref[...].reshape(1, ORDER) + w_lin * start_frac
    )
    scaled = weights[...] * (freq_row * (2.0 / math.pi))
    part_one = scaled.astype(bf16).astype(f32)
    rest = scaled - part_one
    part_two = rest.astype(bf16).astype(f32)
    part_three = (rest - part_two).astype(bf16).astype(f32)
    for at, part in enumerate([part_one, part_one, part_two, part_one, part_two, part_three]):
        weight_stack[at * KROWS : (at + 1) * KROWS, :] = part
    loads[1].wait()
    quarters[...] = dot_first(weight_stack[...].astype(bf16), stacked[...])
    decay_col = as_column(decay_ref[...].reshape(1, CHAN), CHAN)
    small = -2.0 * decay_col
    grown = small * (
        1.0 + small / 2 * (1.0 + small / 3 * (1.0 + small / 4 * (1.0 + small / 5 * (1.0 + small / 6))))
    )
    scaling = jnp.sqrt(grown / (jnp.exp(small * SEQ) - 1.0))
    wide = 256
    for col in range(PART // wide):
        lanes = pl.ds(col * wide, wide)
        sin_val, cos_val = sine_cosine(quarters[:, lanes])
        high, low = high_low(sin_val)
        hidden[0:ORDER, lanes] = high
        hidden[ORDER : 2 * ORDER, lanes] = low
        hidden[2 * ORDER : 3 * ORDER, lanes] = high
        cosines[:, lanes] = cos_val
        times = lax.broadcasted_iota(jnp.int32, (CHAN, wide), 1) + (me * PART + col * wide)
        modul[:, lanes] = jnp.exp(-decay_col * times.astype(f32)) * scaling
    w_high, w_low = high_low(w_second_ref[...])
    w_stack = jnp.concatenate([w_high, w_high, w_low], axis=0)
    filt = dot_first(w_stack, hidden[...]) * modul[...]
    for col in range(ROWS):
        flat_a[pl.ds(col, CHAN, stride=ROWS), :] = filt[:, col * LANES : (col + 1) * LANES]
    send_f[...] = flat_a[...].reshape(CHAN, ROWS, LANES).astype(bf16)
    send_all(send_f, recv_f, 1)

    for at in range(2, 7):
        loads[at].wait()
    wait_all(recv_mg, 0)
    both[:, 0:LANES] = recv_mg[:, 0].reshape(N_ONE, LANES)
    both[:, LANES : 2 * LANES] = recv_mg[:, 1].reshape(N_ONE, LANES)
    chunk = 256

    def turned(rows):
        return twiddle[rows, 0:LANES], twiddle[rows, LANES : 2 * LANES]

    def inverse_part(real, imag, cos_t, sin_t):
        back = dot(jnp.concatenate([real, imag], axis=1).astype(bf16), second_inv[...])
        c_real, c_imag = back[:, :LANES], back[:, LANES:]
        return (
            (c_real * cos_t - c_imag * sin_t).astype(bf16),
            (c_imag * cos_t + c_real * sin_t).astype(bf16),
        )

    def spectrum(a_real, a_imag, cos_t, sin_t):
        b_real = a_real * cos_t + a_imag * sin_t
        b_imag = a_imag * cos_t - a_real * sin_t
        return dot(jnp.concatenate([b_real, b_imag], axis=1).astype(bf16), second[...])

    for at in range(N_ONE // chunk):
        rows = pl.ds(at * chunk, chunk)
        low_rows = pl.ds(N_ONE + at * chunk, chunk)
        cos_t, sin_t = turned(rows)
        a_real = dot(first[rows, :], both[...])
        a_imag = dot(first[low_rows, :], both[...])
        w_spec = spectrum(a_real[:, :LANES], a_imag[:, :LANES], cos_t, sin_t)
        g_spec = spectrum(a_real[:, LANES:], a_imag[:, LANES:], cos_t, sin_t)
        spec_w[rows, :] = w_spec
        spec_g[rows, :] = g_spec
        w_r, w_i, g_r, g_i = w_spec[:, :LANES], w_spec[:, LANES:], g_spec[:, :LANES], g_spec[:, LANES:]
        d_real, d_imag = inverse_part(w_r * g_r + w_i * g_i, w_r * g_i - w_i * g_r, cos_t, sin_t)
        fold_a[rows, :] = d_real
        fold_a[low_rows, :] = d_imag
    send_gf[...] = dot(first_t[...], fold_a[...]).astype(bf16).reshape(CTX, ROWS, LANES)
    send_all(send_gf, recv_gf, 2)

    wait_all(recv_f, 1)
    for at in range(N_ONE // chunk):
        rows = pl.ds(at * chunk, chunk)
        low_rows = pl.ds(N_ONE + at * chunk, chunk)
        cos_t, sin_t = turned(rows)
        filt_c = recv_f[...].reshape(N_ONE, LANES)
        a_real = dot(first[rows, :], filt_c)
        a_imag = dot(first[low_rows, :], filt_c)
        h_spec = spectrum(a_real, a_imag, cos_t, sin_t)
        h_r, h_i = h_spec[:, :LANES], h_spec[:, LANES:]
        w_r, w_i = spec_w[rows, 0:LANES], spec_w[rows, LANES : 2 * LANES]
        g_r, g_i = spec_g[rows, 0:LANES], spec_g[rows, LANES : 2 * LANES]
        d_real, d_imag = inverse_part(h_r * w_r - h_i * w_i, h_r * w_i + h_i * w_r, cos_t, sin_t)
        fold_b[rows, 0:LANES] = d_real
        fold_b[low_rows, 0:LANES] = d_imag
        d_real, d_imag = inverse_part(h_r * g_r + h_i * g_i, h_r * g_i - h_i * g_r, cos_t, sin_t)
        fold_b[rows, LANES : 2 * LANES] = d_real
        fold_b[low_rows, LANES : 2 * LANES] = d_imag
    spread = lax.broadcasted_iota(jnp.int32, (1, CHAN), 1)
    my_skip = jnp.sum(
        jnp.where(spread == me, skip_ref[...].reshape(1, CHAN), 0.0), axis=1, keepdims=True
    )
    direct = dot(first_t[...], fold_b[...]) + my_skip * both[...].astype(f32)
    send_mb[:, 0] = direct[:, :LANES].astype(bf16).reshape(CTX, ROWS, LANES)
    send_mb[:, 1] = direct[:, LANES:].astype(bf16).reshape(CTX, ROWS, LANES)
    send_all(send_mb, recv_mb, 3)

    wait_all(recv_gf, 2)
    flat_a[...] = recv_gf[...].astype(f32).reshape(N_ONE, LANES)
    for col in range(ROWS):
        lanes = pl.ds(col * LANES, LANES)
        part = flat_a[pl.ds(col, CHAN, stride=ROWS), :] * modul[:, lanes]
        high, low = high_low(part)
        grad_mod[0:CHAN, lanes] = high
        grad_mod[CHAN : 2 * CHAN, lanes] = low
    gm_high, gm_low = grad_mod[0:CHAN, :], grad_mod[CHAN : 2 * CHAN, :]
    w_pair = jnp.concatenate([w_high, w_low], axis=0)
    wide_part = dot(w_pair, gm_high)
    grad_hidden = wide_part[:ORDER] + wide_part[ORDER:] + dot(w_high, gm_low)
    high, low = high_low(grad_hidden * cosines[...])
    grad_sin[0:ORDER, :] = high
    grad_sin[ORDER : 2 * ORDER, :] = low
    second_part = dot_last(hidden[0 : 2 * ORDER, :], gm_high)
    second_part = (
        second_part[:ORDER] + second_part[ORDER:] + dot_last(hidden[0:ORDER, :], gm_low)
    )
    loads[7].wait()
    proj = dot_last(pair[...], grad_sin[0:ORDER, :])
    proj = proj[0:KROWS] + proj[48 : 48 + KROWS] + dot_last(pair[0:48, :], grad_sin[ORDER:, :])[0:KROWS]
    p_cos, p_sin = proj[0:BANDS], proj[BANDS : 2 * BANDS]
    p_lin, p_one = proj[2 * BANDS : 2 * BANDS + 1], proj[2 * BANDS + 1 : 2 * BANDS + 2]
    pay[...] = jnp.zeros((CTX * PIECE, LANES), f32)
    pay[0:1, 0:ORDER] = (p_lin + start_frac * p_one) * freq_row
    pay[1 : 1 + BANDS, 0:ORDER] = (p_cos * cos_at - p_sin * sin_at) * freq_row
    pay[1 + BANDS : 1 + 2 * BANDS, 0:ORDER] = (p_cos * sin_at + p_sin * cos_at) * freq_row
    pay[33:34, 0:ORDER] = p_one * freq_row
    pay[34:35, 0:ORDER] = jnp.sum(proj * weights[...], axis=0, keepdims=True)
    pay[40 : 40 + ORDER, 0:CHAN] = second_part
    pay[104:105, 0:CHAN] = skip_row

    for at in range(CTX):
        send_p[at] = pay[at * PIECE : (at + 1) * PIECE, :]
    send_all(send_p, recv_p, 4)
    wait_all(recv_p, 4)
    own = recv_p[0]
    for at in range(1, CTX):
        own = own + recv_p[at]
    piece[...] = own

    def send_slab(step, carry):
        peer = lax.rem(slab + step, SLAB)
        pltpu.make_async_remote_copy(
            src_ref=piece,
            dst_ref=recv_s.at[slab],
            send_sem=send_sem.at[5],
            recv_sem=recv_sem.at[5],
            device_id={"slab": peer},
            device_id_type=MESH,
        ).start()
        return carry

    lax.fori_loop(1, SLAB, send_slab, 0)
    pltpu.make_async_copy(piece, recv_s.at[slab], recv_sem.at[5]).start()

    wait_all(recv_mb, 3)
    flat_a[...] = recv_mb[:, 0].astype(f32).reshape(N_ONE, LANES)
    flat_b[...] = recv_mb[:, 1].astype(f32).reshape(N_ONE, LANES)
    for col in range(ROWS):
        lanes = pl.ds(col * LANES, LANES)
        mid_out[:, lanes] = flat_a[pl.ds(col, CHAN, stride=ROWS), :].astype(bf16)
        back_out[:, lanes] = flat_b[pl.ds(col, CHAN, stride=ROWS), :].astype(bf16)

    wait_all(recv_s, 5)
    total = recv_s[0]
    for at in range(1, SLAB):
        total = total + recv_s[at]
    done[...] = jnp.where(me < 10, total, piece[...])

    def send_done(step, carry):
        peer = lax.rem(me + step, CTX)
        pltpu.make_async_remote_copy(
            src_ref=done,
            dst_ref=recv_d.at[me],
            send_sem=send_sem.at[6],
            recv_sem=recv_sem.at[6],
            device_id={"ctx": peer},
            device_id_type=MESH,
        ).start()
        return carry

    lax.fori_loop(1, CTX, send_done, 0)
    pltpu.make_async_copy(done, recv_d.at[me], recv_sem.at[6]).start()

    wait_sent(send_mg, CTX - 1, 0)
    wait_sent(send_f, CTX - 1, 1)
    wait_sent(send_gf, CTX - 1, 2)
    wait_sent(send_mb, CTX - 1, 3)
    wait_sent(send_p, CTX - 1, 4)
    wait_sent(recv_s, SLAB - 1, 5)
    wait_all(recv_d, 6)
    for at in range(CTX):
        sums_out[at * PIECE : (at + 1) * PIECE, :] = recv_d[at]
    wait_sent(recv_d, CTX - 1, 6)


def last_kernel(
    key_ref,
    value_ref,
    grad_ref,
    mid_ref,
    back_ref,
    sums_ref,
    query_out,
    key_out,
    value_out,
    first_out,
    bias_out,
    freq_out,
    second_out,
    skip_out,
):
    back = back_ref[...].astype(f32)
    query_out[...] = (grad_ref[...].astype(f32) * mid_ref[...].astype(f32)).astype(bf16)
    key_out[...] = (back * value_ref[...].astype(f32)).astype(bf16)
    value_out[...] = (back * key_ref[...].astype(f32)).astype(bf16)
    first_out[...] = sums_ref[0:33, 0:ORDER]
    bias_out[...] = sums_ref[33:34, 0:ORDER].reshape(ORDER)
    freq_out[...] = sums_ref[34:35, 0:ORDER].reshape(ORDER)
    second_out[...] = sums_ref[40 : 40 + ORDER, 0:CHAN]
    skip_out[...] = sums_ref[104:105, 0:CHAN].reshape(CHAN)


def shards(
    query_in,
    key_in,
    value_in,
    grad_out,
    w_first,
    b_first,
    frequency,
    w_second,
    decay_rate,
    skip_gain,
):
    consts = tables()
    vmem = pl.BlockSpec(memory_space=pltpu.VMEM)
    anywhere = pl.BlockSpec(memory_space=pl.ANY)
    block = lambda *dims: pltpu.VMEM(dims, bf16)
    wide = lambda *dims: pltpu.VMEM(dims, f32)
    blocks = (CTX, ROWS, LANES)
    pairs = (CTX, 2, ROWS, LANES)
    rows = jax.ShapeDtypeStruct((CHAN, PART), bf16)
    mid, back, sums = pl.pallas_call(
        main_kernel,
        name="hyena_backward",
        out_shape=(rows, rows, jax.ShapeDtypeStruct((CTX * PIECE, LANES), f32)),
        in_specs=[vmem] * 10 + [anywhere] * 8,
        out_specs=(vmem, vmem, vmem),
        scratch_shapes=[
            block(2 * N_ONE, N_ONE),
            block(N_ONE, 2 * N_ONE),
            block(2 * LANES, 2 * LANES),
            block(2 * LANES, 2 * LANES),
            wide(N_ONE, 2 * LANES),
            block(6 * KROWS, PART),
            block(96, PART),
            wide(2, BANDS, LANES),
            wide(N_ONE, LANES),
            wide(N_ONE, LANES),
            block(*pairs),
            block(*pairs),
            block(*blocks),
            block(*blocks),
            block(*blocks),
            block(*blocks),
            block(*pairs),
            block(*pairs),
            wide(KROWS, ORDER),
            wide(6 * KROWS, ORDER),
            wide(ORDER, PART),
            block(3 * ORDER, PART),
            wide(ORDER, PART),
            wide(CHAN, PART),
            block(N_ONE, 2 * LANES),
            wide(N_ONE, 2 * LANES),
            wide(N_ONE, 2 * LANES),
            block(2 * N_ONE, LANES),
            block(2 * N_ONE, 2 * LANES),
            block(2 * CHAN, PART),
            block(2 * ORDER, PART),
            wide(CTX * PIECE, LANES),
            wide(CTX, PIECE, LANES),
            wide(CTX, PIECE, LANES),
            wide(PIECE, LANES),
            wide(SLAB, PIECE, LANES),
            wide(PIECE, LANES),
            wide(CTX, PIECE, LANES),
            pltpu.SemaphoreType.DMA((8,)),
            pltpu.SemaphoreType.DMA((7,)),
            pltpu.SemaphoreType.DMA((7,)),
        ],
        compiler_params=pltpu.CompilerParams(
            collective_id=0, has_side_effects=True, vmem_limit_bytes=40 * 1024 * 1024
        ),
    )(
        query_in,
        key_in,
        value_in,
        grad_out,
        w_first,
        b_first,
        frequency,
        w_second,
        decay_rate,
        skip_gain,
        *consts,
    )
    return tuple(
        pl.pallas_call(
            last_kernel,
            name="gate_products",
            out_shape=(
                rows,
                rows,
                rows,
                jax.ShapeDtypeStruct((33, ORDER), f32),
                jax.ShapeDtypeStruct((ORDER,), f32),
                jax.ShapeDtypeStruct((ORDER,), f32),
                jax.ShapeDtypeStruct((ORDER, CHAN), f32),
                jax.ShapeDtypeStruct((CHAN,), f32),
            ),
            in_specs=[vmem] * 6,
            out_specs=tuple([vmem] * 8),
        )(key_in, value_in, grad_out, mid, back, sums)
    )


def solution(mesh):
    placed = (
        P("slab", "ctx"),
        P("slab", "ctx"),
        P("slab", "ctx"),
        P("slab", "ctx"),
        P(),
        P(),
        P(),
        P(None, "slab"),
        P("slab"),
        P("slab"),
    )
    return jax.shard_map(
        shards,
        mesh=mesh,
        in_specs=placed,
        out_specs=(
            P("slab", "ctx"),
            P("slab", "ctx"),
            P("slab", "ctx"),
            P(),
            P(),
            P(),
            P(None, "slab"),
            P("slab"),
        ),
        check_vma=False,
    )
```

time: 412 us -> 73.3 us (0.18); the launches traced: 407 us -> 72.7 us
  blocking collectives: 238 us -> 0 us
  matrix products: 73.2 us -> 0 us
  Pallas kernels: 0 us -> 55.6 us
  starting transfers between devices: 35.5 us -> 0 us
  waiting for transfers between devices: 29.3 us -> 0 us
  other arithmetic: 18.9 us -> 0 us
  local copies, waits for them, and re-layouts: 10.5 us -> 16.3 us
    psum x2 -> x0, blocking collectives: 238 us -> none  [the longest x1 129 us: shards(): grad_second, grad_skip = lax.psum((second_part, skip_part), 'ctx')]
    dot_general x17 -> x0, matrix products: 73.2 us -> none  [the longest x12 64.9 us: matmul_high(): return jnp.einsum(form, left, right, precision=lax.Precision.HIGHEST)]
    pallas_call x0 -> x2, Pallas kernels: none -> 55.6 us  [the longest x1 53.6 us: shards(): pl.pallas_call(main_kernel, name='hyena_backward', out_shape=(rows, rows,...]
    all_to_all x6 -> x0, starting transfers between devices: 35.5 us -> none  [the longest x1 10.4 us: shards(): lax.all_to_all(grad_mid, 'ctx', split_axis=0, concat_axis=1, tiled=True)]
    all_to_all x6 -> x0, waiting for transfers between devices: 29.3 us -> none  [the longest x1 7.6 us: shards(): lax.all_to_all(filter_local, 'ctx', split_axis=0, concat_axis=1, tiled=True)]
    unnamed x3 -> x0, other arithmetic: 7.61 us -> none
    unnamed x29 -> x41, local copies, waits for them, and re-layouts: 7.47 us -> 14.9 us
    convert_element_type x5 -> x0, other arithmetic: 4.21 us -> none  [the longest x1 2.12 us: shards(): (back_raw + my_skip[:, None] * grads_c.astype(jnp.float32)).astype(jnp.bf...]
  transfers between devices with their start and end apart: 6 -> 0, of which waited for: 5 -> 0; matrix products, arithmetic and copies ran while one was open for 6% -> 0% of each run, Pallas kernels for 0% -> 0%
where the time goes in v1:
time: 73.3 us; the launch traced here: 72.7 us
  Pallas kernels  55.6 us (76%)
  local copies, waits for them, and re-layouts  16.3 us (22%)
  between operations  0.75 us (1%)
    pallas_call x1, Pallas kernels, shards(): pl.pallas_call(main_kernel, name='hyena_backward', out_shape=(rows, rows,...  53.6 us
    unnamed x41, local copies, waits for them, and re-layouts  14.9 us
    pallas_call x1, Pallas kernels, shards(): pl.pallas_call(last_kernel, name='gate_products', out_shape=(rows, rows,...  1.96 us

profile of v1, /device:TPU:1, one launch (start us, length us, event | category | flops | bytes accessed | tf_op | source)
XLA Modules:
  0.0 72.7 jit_solution(10282802161284792471)
XLA Ops:
  0.6 0.0 copy-start.19
  0.6 0.0 copy-start.18
  0.7 0.0 copy-start.17
  0.7 0.0 copy-start.16
  0.7 0.0 copy-start.15
  0.7 0.8 %copy.26.w_second_ref = f32[64,32]{1,0:T(8,128)S(1)} copy(f32[64,32]{0,1:T(8,128)} %param.25) | data formatting | bytes 16384 | tf_op args[7]
  1.5 0.0 copy-done.19
  1.5 0.0 copy-done.18
  1.5 0.0 copy-done.17
  1.5 0.0 copy-done.16
  1.5 0.0 copy-done.15
  1.6 0.0 copy-start
  1.6 1.2 %copy-done = bf16[512,1024]{1,0:T(8,128)(2,1)S(1)} copy-done((bf16[512,1024]{1,0:T(8,128)(2,1)S(1)}, bf16[512,1024]{1,0:T(8,128)(2,1)}, u32[]{:S(2)}) %copy-start) | copy-done | bytes 1048600
  2.8 0.0 copy-start.1
  2.8 1.2 %copy-done.1 = bf16[1024,512]{1,0:T(8,128)(2,1)S(1)} copy-done((bf16[1024,512]{1,0:T(8,128)(2,1)S(1)}, bf16[1024,512]{1,0:T(8,128)(2,1)}, u32[]{:S(2)}) %copy-start.1) | copy-done | bytes 1048600
  4.0 0.0 copy-start.2
  4.0 1.2 %copy-done.2 = bf16[240,2048]{1,0:T(8,128)(2,1)S(1)} copy-done((bf16[240,2048]{1,0:T(8,128)(2,1)S(1)}, bf16[240,2048]{1,0:T(8,128)(2,1)}, u32[]{:S(2)}) %copy-start.2) | copy-done | bytes 983064
  5.2 0.0 copy-start.3
  5.2 0.9 %copy-done.3 = bf16[32,2048]{1,0:T(8,128)(2,1)S(1)} copy-done((bf16[32,2048]{1,0:T(8,128)(2,1)S(1)}, bf16[32,2048]{1,0:T(8,128)(2,1)}, u32[]{:S(2)}) %copy-start.3) | copy-done | bytes 131096
  6.1 0.0 copy-start.4
  6.1 0.9 %copy-done.4 = bf16[32,2048]{1,0:T(8,128)(2,1)S(1)} copy-done((bf16[32,2048]{1,0:T(8,128)(2,1)S(1)}, bf16[32,2048]{1,0:T(8,128)(2,1)}, u32[]{:S(2)}) %copy-start.4) | copy-done | bytes 131096
  7.0 0.0 copy-start.5
  7.0 0.9 %copy-done.5 = bf16[32,2048]{1,0:T(8,128)(2,1)S(1)} copy-done((bf16[32,2048]{1,0:T(8,128)(2,1)S(1)}, bf16[32,2048]{1,0:T(8,128)(2,1)}, u32[]{:S(2)}) %copy-start.5) | copy-done | bytes 131096
  7.9 0.0 copy-start.6
  7.9 1.0 %copy-done.6 = f32[32,2,16,128]{3,2,1,0:T(8,128)S(1)} copy-done((f32[32,2,16,128]{3,2,1,0:T(8,128)S(1)}, f32[32,2,16,128]{3,2,1,0:T(8,128)}, u32[]{:S(2)}) %copy-start.6) | copy-done | bytes 524312
  9.0 0.0 copy-start.7
  9.0 1.0 %copy-done.7 = f32[512,256]{1,0:T(8,128)S(1)} copy-done((f32[512,256]{1,0:T(8,128)S(1)}, f32[512,256]{1,0:T(8,128)}, u32[]{:S(2)}) %copy-start.7) | copy-done | bytes 524312
  10.0 0.0 copy-start.8
  10.0 1.0 %copy-done.8 = bf16[96,2048]{1,0:T(8,128)(2,1)S(1)} copy-done((bf16[96,2048]{1,0:T(8,128)(2,1)S(1)}, bf16[96,2048]{1,0:T(8,128)(2,1)}, u32[]{:S(2)}) %copy-start.8) | copy-done | bytes 393240
  11.0 0.0 copy-start.9
  11.0 0.9 %copy-done.9 = bf16[32,2048]{1,0:T(8,128)(2,1)S(1)} copy-done((bf16[32,2048]{1,0:T(8,128)(2,1)S(1)}, bf16[32,2048]{1,0:T(8,128)(2,1)}, u32[]{:S(2)}) %copy-start.9) | copy-done | bytes 131096
  11.9 0.0 copy-start.10
  11.9 0.9 %copy-done.10 = bf16[256,256]{1,0:T(8,128)(2,1)S(1)} copy-done((bf16[256,256]{1,0:T(8,128)(2,1)S(1)}, bf16[256,256]{1,0:T(8,128)(2,1)}, u32[]{:S(2)}) %copy-start.10) | copy-done | bytes 131096
  12.8 0.0 copy-start.11
  12.8 0.9 %copy-done.11 = bf16[256,256]{1,0:T(8,128)(2,1)S(1)} copy-done((bf16[256,256]{1,0:T(8,128)(2,1)S(1)}, bf16[256,256]{1,0:T(8,128)(2,1)}, u32[]{:S(2)}) %copy-start.11) | copy-done | bytes 131096
  13.7 53.6 %hyena_backward.1 = (bf16[32,2048]{1,0:T(8,128)(2,1)S(1)}, bf16[32,2048]{1,0:T(8,128)(2,1)S(1)}, f32[128,128]{1,0:T(8,128)S(1)}) custom-call(bf16[32,2048]{1,0:T(8,128)(2,1)S(1)} %copy-done.9, bf16[32,2048]{1,0:T(8,128)(2,1)S(1)} %copy-done.3, bf16[32,2048]{1,0:T(8,128)(2,1)S(1)} %copy-done.4, bf16[32,2048]{1,0:T(8,128)(2,1)S(1)} %copy-done.5, ...), custom_call_target="tpu_custom_call" | custom-call | tf_op jit(solution)/shard_map/hyena_backward/pallas_call | solution.py:530
  67.3 0.0 copy-start.12
  67.4 0.6 copy-done.12
  68.0 0.0 copy-start.13
  68.0 0.6 copy-done.13
  68.6 0.0 copy-start.14
  68.6 0.6 copy-done.14
  69.3 2.0 %gate_products.1 = (bf16[32,2048]{1,0:T(8,128)(2,1)}, bf16[32,2048]{1,0:T(8,128)(2,1)}, bf16[32,2048]{1,0:T(8,128)(2,1)}, f32[33,64]{1,0:T(8,128)}, f32[64]{0:T(...) custom-call(bf16[32,2048]{1,0:T(8,128)(2,1)} %key_ref.3, bf16[32,2048]{1,0:T(8,128)(2,1)} %value_ref.3, ...), custom_call_target="tpu_custom_call" | custom-call | tf_op jit(solution)/shard_map/gate_products/pallas_call | solution.py:596
  71.2 1.4 %copy.27 = f32[64,32]{0,1:T(8,128)} copy(f32[64,32]{1,0:T(8,128)} %get-tuple-element.20) | data formatting | bytes 16384 | tf_op jit(solution)/shard_map/gate_products/pallas_call | solution.py:596
Async XLA Ops:
  0.6 0.9 %copy-start.19 = (f32[32]{0:T(128)S(1)}, f32[32]{0:T(128)}, u32[]{:S(2)}) copy-start(f32[32]{0:T(128)} %skip_ref.1) | copy-start | bytes 388
  0.6 0.9 %copy-start.18 = (f32[32]{0:T(128)S(1)}, f32[32]{0:T(128)}, u32[]{:S(2)}) copy-start(f32[32]{0:T(128)} %decay_ref.1) | copy-start | bytes 388
  0.7 0.9 %copy-start.17 = (f32[64]{0:T(128)S(1)}, f32[64]{0:T(128)}, u32[]{:S(2)}) copy-start(f32[64]{0:T(128)} %freq_ref.1) | copy-start | bytes 772
  0.7 0.9 %copy-start.16 = (f32[64]{0:T(128)S(1)}, f32[64]{0:T(128)}, u32[]{:S(2)}) copy-start(f32[64]{0:T(128)} %b_first_ref.1) | copy-start | bytes 772
  0.7 0.9 %copy-start.15 = (f32[33,64]{1,0:T(8,128)S(1)}, f32[33,64]{1,0:T(8,128)}, u32[]{:S(2)}) copy-start(f32[33,64]{1,0:T(8,128)} %w_first_ref.1) | copy-start | bytes 25348
  1.6 1.2 %copy-start = (bf16[512,1024]{1,0:T(8,128)(2,1)S(1)}, bf16[512,1024]{1,0:T(8,128)(2,1)}, u32[]{:S(2)}) copy-start(bf16[512,1024]{1,0:T(8,128)(2,1)} %constant.17.clone.first_t_hbm) | copy-start | bytes 3145732
  2.8 1.2 %copy-start.1 = (bf16[1024,512]{1,0:T(8,128)(2,1)S(1)}, bf16[1024,512]{1,0:T(8,128)(2,1)}, u32[]{:S(2)}) copy-start(bf16[1024,512]{1,0:T(8,128)(2,1)} %constant.16.clone.first_hbm) | copy-start | bytes 3145732
  4.0 1.2 %copy-start.2 = (bf16[240,2048]{1,0:T(8,128)(2,1)S(1)}, bf16[240,2048]{1,0:T(8,128)(2,1)}, u32[]{:S(2)}) copy-start(bf16[240,2048]{1,0:T(8,128)(2,1)} %constant.21.clone.stacked_hbm) | copy-start | bytes 2949124
  5.2 0.9 %copy-start.3 = (bf16[32,2048]{1,0:T(8,128)(2,1)S(1)}, bf16[32,2048]{1,0:T(8,128)(2,1)}, u32[]{:S(2)}) copy-start(bf16[32,2048]{1,0:T(8,128)(2,1)} %key_ref.3) | copy-start | bytes 393220
  6.1 0.9 %copy-start.4 = (bf16[32,2048]{1,0:T(8,128)(2,1)S(1)}, bf16[32,2048]{1,0:T(8,128)(2,1)}, u32[]{:S(2)}) copy-start(bf16[32,2048]{1,0:T(8,128)(2,1)} %value_ref.3) | copy-start | bytes 393220
  7.0 0.9 %copy-start.5 = (bf16[32,2048]{1,0:T(8,128)(2,1)S(1)}, bf16[32,2048]{1,0:T(8,128)(2,1)}, u32[]{:S(2)}) copy-start(bf16[32,2048]{1,0:T(8,128)(2,1)} %grad_ref.3) | copy-start | bytes 393220
  7.9 1.0 %copy-start.6 = (f32[32,2,16,128]{3,2,1,0:T(8,128)S(1)}, f32[32,2,16,128]{3,2,1,0:T(8,128)}, u32[]{:S(2)}) copy-start(f32[32,2,16,128]{3,2,1,0:T(8,128)} %constant.23.clone.rot_hbm) | copy-start | bytes 1572868
  9.0 1.0 %copy-start.7 = (f32[512,256]{1,0:T(8,128)S(1)}, f32[512,256]{1,0:T(8,128)}, u32[]{:S(2)}) copy-start(f32[512,256]{1,0:T(8,128)} %constant.20.clone.twiddle_hbm) | copy-start | bytes 1572868
  10.0 1.0 %copy-start.8 = (bf16[96,2048]{1,0:T(8,128)(2,1)S(1)}, bf16[96,2048]{1,0:T(8,128)(2,1)}, u32[]{:S(2)}) copy-start(bf16[96,2048]{1,0:T(8,128)(2,1)} %constant.22.clone.pair_hbm) | copy-start | bytes 1179652
  11.0 0.9 %copy-start.9 = (bf16[32,2048]{1,0:T(8,128)(2,1)S(1)}, bf16[32,2048]{1,0:T(8,128)(2,1)}, u32[]{:S(2)}) copy-start(bf16[32,2048]{1,0:T(8,128)(2,1)} %query_ref.1) | copy-start | bytes 393220
  11.9 0.9 %copy-start.10 = (bf16[256,256]{1,0:T(8,128)(2,1)S(1)}, bf16[256,256]{1,0:T(8,128)(2,1)}, u32[]{:S(2)}) copy-start(bf16[256,256]{1,0:T(8,128)(2,1)} %constant.19.clone.second_inv_hbm) | copy-start | bytes 393220
  12.8 0.9 %copy-start.11 = (bf16[256,256]{1,0:T(8,128)(2,1)S(1)}, bf16[256,256]{1,0:T(8,128)(2,1)}, u32[]{:S(2)}) copy-start(bf16[256,256]{1,0:T(8,128)(2,1)} %constant.18.clone.second_hbm) | copy-start | bytes 393220
  67.3 0.6 copy-start.12
  68.0 0.6 copy-start.13
  68.6 0.6 copy-start.14

commit v2 on v1

--- a/solution.py
+++ b/solution.py
@@ -20,7 +20,7 @@
 N_ONE = SEQ // LANES
 ORDER = 64
 KROWS = 40
-PIECE = 4
+PIECE = 2
 
 MESH = pl.DeviceIdType.MESH
 f32, bf16 = jnp.float32, jnp.bfloat16
@@ -100,9 +100,11 @@
     return jnp.sum(jnp.where(eye(count), spread, 0.0), axis=1, keepdims=True)
 
 
-def as_row(column, count):
-    spread = jnp.broadcast_to(column, (count, count))
-    return jnp.sum(jnp.where(eye(count), spread, 0.0), axis=0, keepdims=True)
+def in_upper_lanes(column, count):
+    rows = lax.broadcasted_iota(jnp.int32, (count, LANES), 0)
+    lanes = lax.broadcasted_iota(jnp.int32, (count, LANES), 1)
+    spread = jnp.broadcast_to(column, (count, LANES))
+    return jnp.sum(jnp.where(lanes == rows + ORDER, spread, 0.0), axis=0, keepdims=True)
 
 
 def sine_cosine(quarters):
@@ -126,6 +128,28 @@
 
 
 def main_kernel(
+    query_hbm,
+    key_hbm,
+    value_hbm,
+    grad_hbm,
+    w_first_hbm,
+    b_first_hbm,
+    freq_hbm,
+    w_second_hbm,
+    decay_hbm,
+    skip_hbm,
+    first_hbm,
+    first_t_hbm,
+    second_hbm,
+    second_inv_hbm,
+    twiddle_hbm,
+    stacked_hbm,
+    pair_hbm,
+    rot_hbm,
+    query_out,
+    key_out,
+    value_out,
+    sums_out,
     query_ref,
     key_ref,
     value_ref,
@@ -136,17 +160,6 @@
     w_second_ref,
     decay_ref,
     skip_ref,
-    first_hbm,
-    first_t_hbm,
-    second_hbm,
-    second_inv_hbm,
-    twiddle_hbm,
-    stacked_hbm,
-    pair_hbm,
-    rot_hbm,
-    mid_out,
-    back_out,
-    sums_out,
     first,
     first_t,
     second,
@@ -206,15 +219,39 @@
         )
         return carry
 
+    lax.fori_loop(1, SLAB, greet_slab, 0)
     lax.fori_loop(1, CTX, greet_ctx, 0)
-    lax.fori_loop(1, SLAB, greet_slab, 0)
-
-    loads = [
-        pltpu.make_async_copy(source, target, table_sem.at[at])
+
+    def load(source, target, at):
+        copy = pltpu.make_async_copy(source, target, table_sem.at[at])
+        copy.start()
+        return copy
+
+    gates = [
+        load(source, target, at)
+        for at, (source, target) in enumerate(
+            [(key_hbm, key_ref), (value_hbm, value_ref), (grad_hbm, grad_ref), (query_hbm, query_ref)]
+        )
+    ]
+    layers = [
+        load(source, target, 4 + at)
         for at, (source, target) in enumerate(
             [
                 (rot_hbm.at[me], rot),
+                (w_first_hbm, w_first_ref),
+                (b_first_hbm, b_first_ref),
+                (freq_hbm, freq_ref),
+                (w_second_hbm, w_second_ref),
+                (decay_hbm, decay_ref),
+                (skip_hbm, skip_ref),
                 (stacked_hbm, stacked),
+            ]
+        )
+    ]
+    transforms = [
+        load(source, target, 12 + at)
+        for at, (source, target) in enumerate(
+            [
                 (first_hbm, first),
                 (second_hbm, second),
                 (second_inv_hbm, second_inv),
@@ -224,8 +261,10 @@
             ]
         )
     ]
-    for load in loads:
-        load.start()
+
+    def wait_loads(copies):
+        for copy in copies:
+            copy.wait()
 
     def send_all(source, target, at):
         def body(step, carry):
@@ -250,6 +289,7 @@
         part = source.at[pl.ds(0, count)]
         pltpu.make_async_copy(part, part, send_sem.at[at]).wait()
 
+    wait_loads(gates)
     skip_acc = jnp.zeros((CHAN, LANES), f32)
     for col in range(ROWS):
         lanes = pl.ds(col * LANES, LANES)
@@ -262,12 +302,9 @@
         skip_acc = skip_acc + mixed * mid
     send_mg[:, 0] = flat_a[...].reshape(CHAN, ROWS, LANES).astype(bf16)
     send_mg[:, 1] = flat_b[...].reshape(CHAN, ROWS, LANES).astype(bf16)
-    skip_row = as_row(jnp.sum(skip_acc, axis=1, keepdims=True), CHAN)
-
-    pl.semaphore_wait(barrier, CTX + SLAB - 2)
-    send_all(send_mg, recv_mg, 0)
-
-    loads[0].wait()
+    skip_row = in_upper_lanes(jnp.sum(skip_acc, axis=1, keepdims=True), CHAN)
+
+    wait_loads(layers)
     cos_at, sin_at = rot[0][:, :ORDER], rot[1][:, :ORDER]
     w_lin = w_first_ref[0:1, :]
     w_cos = w_first_ref[1 : 1 + BANDS, :]
@@ -288,7 +325,6 @@
     part_three = (rest - part_two).astype(bf16).astype(f32)
     for at, part in enumerate([part_one, part_one, part_two, part_one, part_two, part_three]):
         weight_stack[at * KROWS : (at + 1) * KROWS, :] = part
-    loads[1].wait()
     quarters[...] = dot_first(weight_stack[...].astype(bf16), stacked[...])
     decay_col = as_column(decay_ref[...].reshape(1, CHAN), CHAN)
     small = -2.0 * decay_col
@@ -303,20 +339,21 @@
         high, low = high_low(sin_val)
         hidden[0:ORDER, lanes] = high
         hidden[ORDER : 2 * ORDER, lanes] = low
-        hidden[2 * ORDER : 3 * ORDER, lanes] = high
         cosines[:, lanes] = cos_val
         times = lax.broadcasted_iota(jnp.int32, (CHAN, wide), 1) + (me * PART + col * wide)
         modul[:, lanes] = jnp.exp(-decay_col * times.astype(f32)) * scaling
     w_high, w_low = high_low(w_second_ref[...])
-    w_stack = jnp.concatenate([w_high, w_high, w_low], axis=0)
-    filt = dot_first(w_stack, hidden[...]) * modul[...]
+    filt = dot(jnp.concatenate([w_high, w_low], axis=0), hidden[0:ORDER, :])
+    filt = filt[:CHAN] + filt[CHAN:] + dot(w_high, hidden[ORDER : 2 * ORDER, :])
+    filt = filt * modul[...]
     for col in range(ROWS):
         flat_a[pl.ds(col, CHAN, stride=ROWS), :] = filt[:, col * LANES : (col + 1) * LANES]
     send_f[...] = flat_a[...].reshape(CHAN, ROWS, LANES).astype(bf16)
-    send_all(send_f, recv_f, 1)
-
-    for at in range(2, 7):
-        loads[at].wait()
+
+    pl.semaphore_wait(barrier, CTX + SLAB - 2)
+    send_all(send_mg, recv_mg, 0)
+
+    wait_loads(transforms)
     wait_all(recv_mg, 0)
     both[:, 0:LANES] = recv_mg[:, 0].reshape(N_ONE, LANES)
     both[:, LANES : 2 * LANES] = recv_mg[:, 1].reshape(N_ONE, LANES)
@@ -354,6 +391,45 @@
         fold_a[low_rows, :] = d_imag
     send_gf[...] = dot(first_t[...], fold_a[...]).astype(bf16).reshape(CTX, ROWS, LANES)
     send_all(send_gf, recv_gf, 2)
+    send_all(send_f, recv_f, 1)
+
+    wait_all(recv_gf, 2)
+    flat_a[...] = recv_gf[...].astype(f32).reshape(N_ONE, LANES)
+    for col in range(ROWS):
+        lanes = pl.ds(col * LANES, LANES)
+        part = flat_a[pl.ds(col, CHAN, stride=ROWS), :] * modul[:, lanes]
+        high, low = high_low(part)
+        grad_mod[0:CHAN, lanes] = high
+        grad_mod[CHAN : 2 * CHAN, lanes] = low
+        grad_mod[2 * CHAN : 3 * CHAN, lanes] = high
+    grad_hidden = dot_first(jnp.concatenate([w_high, w_high, w_low], axis=0), grad_mod[...])
+    high, low = high_low(grad_hidden * cosines[...])
+    grad_sin[0:ORDER, :] = high
+    grad_sin[ORDER : 2 * ORDER, :] = low
+    second_part = dot_last(grad_mod[0 : 2 * CHAN, :], hidden[...])
+    high_part = second_part[:CHAN]
+    low_part = jnp.where(
+        lax.broadcasted_iota(jnp.int32, (CHAN, LANES), 1) < ORDER, second_part[CHAN:], 0.0
+    )
+    second_part = high_part + low_part
+    second_part = second_part + pltpu.roll(second_part, ORDER, 1)
+    proj = dot_last(pair[...], grad_sin[0:ORDER, :])
+    proj = proj[0:KROWS] + proj[48 : 48 + KROWS] + dot_last(pair[0:48, :], grad_sin[ORDER:, :])[0:KROWS]
+    p_cos, p_sin = proj[0:BANDS], proj[BANDS : 2 * BANDS]
+    p_lin, p_one = proj[2 * BANDS : 2 * BANDS + 1], proj[2 * BANDS + 1 : 2 * BANDS + 2]
+    pay[...] = jnp.zeros((CTX * PIECE, LANES), f32)
+    upper = lax.broadcasted_iota(jnp.int32, (CHAN, LANES), 1) >= ORDER
+    pay[0:CHAN, :] = jnp.where(upper, second_part, 0.0)
+    pay[CHAN : CHAN + 1, :] = skip_row
+    pay[0:1, 0:ORDER] = (p_lin + start_frac * p_one) * freq_row
+    pay[1 : 1 + BANDS, 0:ORDER] = (p_cos * cos_at - p_sin * sin_at) * freq_row
+    pay[1 + BANDS : 1 + 2 * BANDS, 0:ORDER] = (p_cos * sin_at + p_sin * cos_at) * freq_row
+    pay[33:34, 0:ORDER] = p_one * freq_row
+    pay[34:35, 0:ORDER] = jnp.sum(proj * weights[...], axis=0, keepdims=True)
+
+    for at in range(CTX):
+        send_p[at] = pay[at * PIECE : (at + 1) * PIECE, :]
+    send_all(send_p, recv_p, 4)
 
     wait_all(recv_f, 1)
     for at in range(N_ONE // chunk):
@@ -380,44 +456,8 @@
     direct = dot(first_t[...], fold_b[...]) + my_skip * both[...].astype(f32)
     send_mb[:, 0] = direct[:, :LANES].astype(bf16).reshape(CTX, ROWS, LANES)
     send_mb[:, 1] = direct[:, LANES:].astype(bf16).reshape(CTX, ROWS, LANES)
-    send_all(send_mb, recv_mb, 3)
-
-    wait_all(recv_gf, 2)
-    flat_a[...] = recv_gf[...].astype(f32).reshape(N_ONE, LANES)
-    for col in range(ROWS):
-        lanes = pl.ds(col * LANES, LANES)
-        part = flat_a[pl.ds(col, CHAN, stride=ROWS), :] * modul[:, lanes]
-        high, low = high_low(part)
-        grad_mod[0:CHAN, lanes] = high
-        grad_mod[CHAN : 2 * CHAN, lanes] = low
-    gm_high, gm_low = grad_mod[0:CHAN, :], grad_mod[CHAN : 2 * CHAN, :]
-    w_pair = jnp.concatenate([w_high, w_low], axis=0)
-    wide_part = dot(w_pair, gm_high)
-    grad_hidden = wide_part[:ORDER] + wide_part[ORDER:] + dot(w_high, gm_low)
-    high, low = high_low(grad_hidden * cosines[...])
-    grad_sin[0:ORDER, :] = high
-    grad_sin[ORDER : 2 * ORDER, :] = low
-    second_part = dot_last(hidden[0 : 2 * ORDER, :], gm_high)
-    second_part = (
-        second_part[:ORDER] + second_part[ORDER:] + dot_last(hidden[0:ORDER, :], gm_low)
-    )
-    loads[7].wait()
-    proj = dot_last(pair[...], grad_sin[0:ORDER, :])
-    proj = proj[0:KROWS] + proj[48 : 48 + KROWS] + dot_last(pair[0:48, :], grad_sin[ORDER:, :])[0:KROWS]
-    p_cos, p_sin = proj[0:BANDS], proj[BANDS : 2 * BANDS]
-    p_lin, p_one = proj[2 * BANDS : 2 * BANDS + 1], proj[2 * BANDS + 1 : 2 * BANDS + 2]
-    pay[...] = jnp.zeros((CTX * PIECE, LANES), f32)
-    pay[0:1, 0:ORDER] = (p_lin + start_frac * p_one) * freq_row
-    pay[1 : 1 + BANDS, 0:ORDER] = (p_cos * cos_at - p_sin * sin_at) * freq_row
-    pay[1 + BANDS : 1 + 2 * BANDS, 0:ORDER] = (p_cos * sin_at + p_sin * cos_at) * freq_row
-    pay[33:34, 0:ORDER] = p_one * freq_row
-    pay[34:35, 0:ORDER] = jnp.sum(proj * weights[...], axis=0, keepdims=True)
-    pay[40 : 40 + ORDER, 0:CHAN] = second_part
-    pay[104:105, 0:CHAN] = skip_row
-
-    for at in range(CTX):
-        send_p[at] = pay[at * PIECE : (at + 1) * PIECE, :]
-    send_all(send_p, recv_p, 4)
+
+
     wait_all(recv_p, 4)
     own = recv_p[0]
     for at in range(1, CTX):
@@ -438,20 +478,14 @@
 
     lax.fori_loop(1, SLAB, send_slab, 0)
     pltpu.make_async_copy(piece, recv_s.at[slab], recv_sem.at[5]).start()
-
-    wait_all(recv_mb, 3)
-    flat_a[...] = recv_mb[:, 0].astype(f32).reshape(N_ONE, LANES)
-    flat_b[...] = recv_mb[:, 1].astype(f32).reshape(N_ONE, LANES)
-    for col in range(ROWS):
-        lanes = pl.ds(col * LANES, LANES)
-        mid_out[:, lanes] = flat_a[pl.ds(col, CHAN, stride=ROWS), :].astype(bf16)
-        back_out[:, lanes] = flat_b[pl.ds(col, CHAN, stride=ROWS), :].astype(bf16)
+    send_all(send_mb, recv_mb, 3)
 
     wait_all(recv_s, 5)
     total = recv_s[0]
     for at in range(1, SLAB):
         total = total + recv_s[at]
-    done[...] = jnp.where(me < 10, total, piece[...])
+    summed = lax.broadcasted_iota(jnp.int32, (PIECE, LANES), 1) < ORDER
+    done[...] = jnp.where(summed, total, piece[...])
 
     def send_done(step, carry):
         peer = lax.rem(me + step, CTX)
@@ -468,6 +502,17 @@
     lax.fori_loop(1, CTX, send_done, 0)
     pltpu.make_async_copy(done, recv_d.at[me], recv_sem.at[6]).start()
 
+    wait_all(recv_mb, 3)
+    flat_a[...] = recv_mb[:, 0].astype(f32).reshape(N_ONE, LANES)
+    flat_b[...] = recv_mb[:, 1].astype(f32).reshape(N_ONE, LANES)
+    for col in range(ROWS):
+        lanes = pl.ds(col * LANES, LANES)
+        mid = flat_a[pl.ds(col, CHAN, stride=ROWS), :]
+        back = flat_b[pl.ds(col, CHAN, stride=ROWS), :]
+        query_out[:, lanes] = (grad_ref[:, lanes].astype(f32) * mid).astype(bf16)
+        key_out[:, lanes] = (back * value_ref[:, lanes].astype(f32)).astype(bf16)
+        value_out[:, lanes] = (back * key_ref[:, lanes].astype(f32)).astype(bf16)
+
     wait_sent(send_mg, CTX - 1, 0)
     wait_sent(send_f, CTX - 1, 1)
     wait_sent(send_gf, CTX - 1, 2)
@@ -481,11 +526,9 @@
 
 
 def last_kernel(
+    query_ref,
     key_ref,
     value_ref,
-    grad_ref,
-    mid_ref,
-    back_ref,
     sums_ref,
     query_out,
     key_out,
@@ -495,16 +538,23 @@
     freq_out,
     second_out,
     skip_out,
+    sem,
 ):
-    back = back_ref[...].astype(f32)
-    query_out[...] = (grad_ref[...].astype(f32) * mid_ref[...].astype(f32)).astype(bf16)
-    key_out[...] = (back * value_ref[...].astype(f32)).astype(bf16)
-    value_out[...] = (back * key_ref[...].astype(f32)).astype(bf16)
+    stores = [
+        pltpu.make_async_copy(source, target, sem.at[at])
+        for at, (source, target) in enumerate(
+            [(query_ref, query_out), (key_ref, key_out), (value_ref, value_out)]
+        )
+    ]
+    for store in stores:
+        store.start()
     first_out[...] = sums_ref[0:33, 0:ORDER]
     bias_out[...] = sums_ref[33:34, 0:ORDER].reshape(ORDER)
     freq_out[...] = sums_ref[34:35, 0:ORDER].reshape(ORDER)
-    second_out[...] = sums_ref[40 : 40 + ORDER, 0:CHAN]
-    skip_out[...] = sums_ref[104:105, 0:CHAN].reshape(CHAN)
+    second_out[...] = sums_ref[0:CHAN, ORDER : 2 * ORDER]
+    skip_out[...] = sums_ref[CHAN : CHAN + 1, ORDER : ORDER + CHAN].reshape(CHAN)
+    for store in stores:
+        store.wait()
 
 
 def shards(
@@ -521,19 +571,30 @@
 ):
     consts = tables()
     vmem = pl.BlockSpec(memory_space=pltpu.VMEM)
-    anywhere = pl.BlockSpec(memory_space=pl.ANY)
+    hbm = pl.BlockSpec(memory_space=pltpu.HBM)
     block = lambda *dims: pltpu.VMEM(dims, bf16)
     wide = lambda *dims: pltpu.VMEM(dims, f32)
     blocks = (CTX, ROWS, LANES)
     pairs = (CTX, 2, ROWS, LANES)
     rows = jax.ShapeDtypeStruct((CHAN, PART), bf16)
-    mid, back, sums = pl.pallas_call(
+    sums_shape = jax.ShapeDtypeStruct((CTX * PIECE, LANES), f32)
+    query_g, key_g, value_g, sums = pl.pallas_call(
         main_kernel,
         name="hyena_backward",
-        out_shape=(rows, rows, jax.ShapeDtypeStruct((CTX * PIECE, LANES), f32)),
-        in_specs=[vmem] * 10 + [anywhere] * 8,
-        out_specs=(vmem, vmem, vmem),
+        out_shape=(rows, rows, rows, sums_shape),
+        in_specs=[hbm] * 18,
+        out_specs=(vmem, vmem, vmem, vmem),
         scratch_shapes=[
+            block(CHAN, PART),
+            block(CHAN, PART),
+            block(CHAN, PART),
+            block(CHAN, PART),
+            wide(33, ORDER),
+            wide(ORDER),
+            wide(ORDER),
+            wide(CHAN, ORDER),
+            wide(CHAN),
+            wide(CHAN),
             block(2 * N_ONE, N_ONE),
             block(N_ONE, 2 * N_ONE),
             block(2 * LANES, 2 * LANES),
@@ -555,7 +616,7 @@
             wide(KROWS, ORDER),
             wide(6 * KROWS, ORDER),
             wide(ORDER, PART),
-            block(3 * ORDER, PART),
+            block(2 * ORDER, PART),
             wide(ORDER, PART),
             wide(CHAN, PART),
             block(N_ONE, 2 * LANES),
@@ -563,7 +624,7 @@
             wide(N_ONE, 2 * LANES),
             block(2 * N_ONE, LANES),
             block(2 * N_ONE, 2 * LANES),
-            block(2 * CHAN, PART),
+            block(3 * CHAN, PART),
             block(2 * ORDER, PART),
             wide(CTX * PIECE, LANES),
             wide(CTX, PIECE, LANES),
@@ -572,7 +633,7 @@
             wide(SLAB, PIECE, LANES),
             wide(PIECE, LANES),
             wide(CTX, PIECE, LANES),
-            pltpu.SemaphoreType.DMA((8,)),
+            pltpu.SemaphoreType.DMA((18,)),
             pltpu.SemaphoreType.DMA((7,)),
             pltpu.SemaphoreType.DMA((7,)),
         ],
@@ -580,6 +641,7 @@
             collective_id=0, has_side_effects=True, vmem_limit_bytes=40 * 1024 * 1024
         ),
     )(
+        *[pltpu.with_memory_space_constraint(held, pltpu.HBM) for held in (
         query_in,
         key_in,
         value_in,
@@ -587,29 +649,32 @@
         w_first,
         b_first,
         frequency,
-        w_second,
+        w_second.T,
         decay_rate,
         skip_gain,
         *consts,
-    )
-    return tuple(
-        pl.pallas_call(
-            last_kernel,
-            name="gate_products",
-            out_shape=(
-                rows,
-                rows,
-                rows,
-                jax.ShapeDtypeStruct((33, ORDER), f32),
-                jax.ShapeDtypeStruct((ORDER,), f32),
-                jax.ShapeDtypeStruct((ORDER,), f32),
-                jax.ShapeDtypeStruct((ORDER, CHAN), f32),
-                jax.ShapeDtypeStruct((CHAN,), f32),
-            ),
-            in_specs=[vmem] * 6,
-            out_specs=tuple([vmem] * 8),
-        )(key_in, value_in, grad_out, mid, back, sums)
-    )
+        )]
+    )
+    vector = lambda count: jax.ShapeDtypeStruct((count,), f32)
+    outs = pl.pallas_call(
+        last_kernel,
+        name="results",
+        out_shape=(
+            rows,
+            rows,
+            rows,
+            jax.ShapeDtypeStruct((33, ORDER), f32),
+            vector(ORDER),
+            vector(ORDER),
+            jax.ShapeDtypeStruct((CHAN, ORDER), f32),
+            vector(CHAN),
+        ),
+        in_specs=[vmem] * 4,
+        out_specs=(hbm, hbm, hbm, vmem, vmem, vmem, vmem, vmem),
+        scratch_shapes=[pltpu.SemaphoreType.DMA((3,))],
+        compiler_params=pltpu.CompilerParams(vmem_limit_bytes=56 * 1024 * 1024),
+    )(*[pltpu.with_memory_space_constraint(held, pltpu.VMEM) for held in (query_g, key_g, value_g, sums)])
+    return (*outs[:6], outs[6].T, outs[7])
 
 
 def solution(mesh):

time: 73.3 us -> 55 us (0.75)
  local copies, waits for them, and re-layouts: 16.3 us -> 0 us
  Pallas kernels: 55.6 us -> 54.2 us
    unnamed x41 -> x0, local copies, waits for them, and re-layouts: 14.9 us -> none
    pallas_call x1 -> x0, local copies, waits for them, and re-layouts: 1.44 us -> none  [shards(): pl.pallas_call(last_kernel, name='gate_products', out_shape=(rows, rows,...]
    pallas_call x1, Pallas kernels: 53.6 us -> 52.8 us  [shards(): pl.pallas_call(main_kernel, name='hyena_backward', out_shape=(rows, rows,...]
where the time goes in v2:
time: 55 us; the launch traced here: 54.9 us
  Pallas kernels  54.2 us (99%)
  between operations  0.64 us (1%)
    pallas_call x1, Pallas kernels, shards(): pl.pallas_call(main_kernel, name='hyena_backward', out_shape=(rows, rows,...  52.8 us
    pallas_call x1, Pallas kernels, shards(): pl.pallas_call(last_kernel, name='results', out_shape=(rows, rows, rows,...  1.39 us

profile of v2, /device:TPU:1, one launch (start us, length us, event | category | flops | bytes accessed | tf_op | source)
XLA Modules:
  0.0 54.9 jit_solution(13105974320454745003)
XLA Ops:
  0.6 52.8 %hyena_backward.1 = (bf16[32,2048]{1,0:T(8,128)(2,1)S(1)}, bf16[32,2048]{1,0:T(8,128)(2,1)S(1)}, bf16[32,2048]{1,0:T(8,128)(2,1)S(1)}, f32[64,128]{1,0:T(8,128)S(1)}) custom-call(bf16[32,2048]{1,0:T(8,128)(2,1)} %query_hbm.1, bf16[32,2048]{1,0:T(8,128)(2,1)} %key_hbm.1, bf16[32,2048]{1,0:T(8,128)(2,1)} %value_hbm.1, bf16[32,2048]{1,0:T(8,128)(2,1)} %grad_hbm.1, ...), custom_call_target="tpu_custom_call" | custom-call | tf_op jit(solution)/shard_map/hyena_backward/pallas_call | solution.py:581
  53.5 1.4 %results.1 = (bf16[32,2048]{1,0:T(8,128)(2,1)}, bf16[32,2048]{1,0:T(8,128)(2,1)}, bf16[32,2048]{1,0:T(8,128)(2,1)}, f32[33,64]{1,0:T(8,128)}, f32[64]{0:T(128)},...) custom-call(bf16[32,2048]{1,0:T(8,128)(2,1)S(1)} %get-tuple-element.20.query_ref, ...), custom_call_target="tpu_custom_call" | custom-call | tf_op jit(solution)/shard_map/results/pallas_call | solution.py:659

commit v3 on v2

--- a/solution.py
+++ b/solution.py
@@ -20,7 +20,9 @@
 N_ONE = SEQ // LANES
 ORDER = 64
 KROWS = 40
-PIECE = 2
+Z_LO, Z_HI, Y_ALL, FLAT = 4, 4, 4, 8
+PLANE = Y_ALL * FLAT
+Z_ALL = Z_HI * Z_LO
 
 MESH = pl.DeviceIdType.MESH
 f32, bf16 = jnp.float32, jnp.bfloat16
@@ -100,11 +102,9 @@
     return jnp.sum(jnp.where(eye(count), spread, 0.0), axis=1, keepdims=True)
 
 
-def in_upper_lanes(column, count):
-    rows = lax.broadcasted_iota(jnp.int32, (count, LANES), 0)
-    lanes = lax.broadcasted_iota(jnp.int32, (count, LANES), 1)
-    spread = jnp.broadcast_to(column, (count, LANES))
-    return jnp.sum(jnp.where(lanes == rows + ORDER, spread, 0.0), axis=0, keepdims=True)
+def as_row(column, count):
+    spread = jnp.broadcast_to(column, (count, count))
+    return jnp.sum(jnp.where(eye(count), spread, 0.0), axis=0, keepdims=True)
 
 
 def sine_cosine(quarters):
@@ -191,16 +191,21 @@
     fold_b,
     grad_mod,
     grad_sin,
+    spare,
     pay,
-    send_p,
     recv_p,
     piece,
     recv_s,
     done,
     recv_d,
+    pay_own,
+    recv_own,
+    done_own,
+    all_own,
     table_sem,
     send_sem,
     recv_sem,
+    entered,
 ):
     me = lax.axis_index("ctx")
     slab = lax.axis_index("slab")
@@ -213,14 +218,33 @@
         )
         return carry
 
-    def greet_slab(step, carry):
-        pl.semaphore_signal(
-            barrier, inc=1, device_id={"slab": lax.rem(slab + step, SLAB)}, device_id_type=MESH
-        )
-        return carry
-
-    lax.fori_loop(1, SLAB, greet_slab, 0)
+    zl, flat = lax.div(me, FLAT), lax.rem(me, FLAT)
+    zh, yy = lax.div(slab, Y_ALL), lax.rem(slab, Y_ALL)
+    depth = zh * Z_LO + zl
+    at_plane = yy * FLAT + flat
+
+    def in_plane(at):
+        return {
+            "ctx": zl * FLAT + lax.rem(at, FLAT),
+            "slab": zh * Y_ALL + lax.div(at, FLAT),
+        }
+
+    def in_column(at):
+        return {
+            "ctx": lax.rem(at, Z_LO) * FLAT + flat,
+            "slab": lax.div(at, Z_LO) * Y_ALL + yy,
+        }
+
+    def signal_each(semaphore, place, first_at, last_at):
+        def body(at, carry):
+            pl.semaphore_signal(semaphore, inc=1, device_id=place(at), device_id_type=MESH)
+            return carry
+
+        lax.fori_loop(first_at, last_at, body, 0)
+
     lax.fori_loop(1, CTX, greet_ctx, 0)
+    signal_each(barrier, in_plane, (yy + 1) * FLAT, PLANE)
+    signal_each(barrier, in_column, (zh + 1) * Z_LO, Z_ALL)
 
     def load(source, target, at):
         copy = pltpu.make_async_copy(source, target, table_sem.at[at])
@@ -302,7 +326,7 @@
         skip_acc = skip_acc + mixed * mid
     send_mg[:, 0] = flat_a[...].reshape(CHAN, ROWS, LANES).astype(bf16)
     send_mg[:, 1] = flat_b[...].reshape(CHAN, ROWS, LANES).astype(bf16)
-    skip_row = in_upper_lanes(jnp.sum(skip_acc, axis=1, keepdims=True), CHAN)
+    skip_sum = jnp.sum(skip_acc, axis=1, keepdims=True)
 
     wait_loads(layers)
     cos_at, sin_at = rot[0][:, :ORDER], rot[1][:, :ORDER]
@@ -350,8 +374,10 @@
         flat_a[pl.ds(col, CHAN, stride=ROWS), :] = filt[:, col * LANES : (col + 1) * LANES]
     send_f[...] = flat_a[...].reshape(CHAN, ROWS, LANES).astype(bf16)
 
-    pl.semaphore_wait(barrier, CTX + SLAB - 2)
+    pl.semaphore_wait(barrier, CTX - 1 + yy * FLAT + zh * Z_LO)
     send_all(send_mg, recv_mg, 0)
+    signal_each(entered, in_plane, 0, yy * FLAT)
+    signal_each(entered, in_column, 0, zh * Z_LO)
 
     wait_loads(transforms)
     wait_all(recv_mg, 0)
@@ -391,7 +417,6 @@
         fold_a[low_rows, :] = d_imag
     send_gf[...] = dot(first_t[...], fold_a[...]).astype(bf16).reshape(CTX, ROWS, LANES)
     send_all(send_gf, recv_gf, 2)
-    send_all(send_f, recv_f, 1)
 
     wait_all(recv_gf, 2)
     flat_a[...] = recv_gf[...].astype(f32).reshape(N_ONE, LANES)
@@ -417,19 +442,73 @@
     proj = proj[0:KROWS] + proj[48 : 48 + KROWS] + dot_last(pair[0:48, :], grad_sin[ORDER:, :])[0:KROWS]
     p_cos, p_sin = proj[0:BANDS], proj[BANDS : 2 * BANDS]
     p_lin, p_one = proj[2 * BANDS : 2 * BANDS + 1], proj[2 * BANDS + 1 : 2 * BANDS + 2]
-    pay[...] = jnp.zeros((CTX * PIECE, LANES), f32)
-    upper = lax.broadcasted_iota(jnp.int32, (CHAN, LANES), 1) >= ORDER
-    pay[0:CHAN, :] = jnp.where(upper, second_part, 0.0)
-    pay[CHAN : CHAN + 1, :] = skip_row
-    pay[0:1, 0:ORDER] = (p_lin + start_frac * p_one) * freq_row
-    pay[1 : 1 + BANDS, 0:ORDER] = (p_cos * cos_at - p_sin * sin_at) * freq_row
-    pay[1 + BANDS : 1 + 2 * BANDS, 0:ORDER] = (p_cos * sin_at + p_sin * cos_at) * freq_row
-    pay[33:34, 0:ORDER] = p_one * freq_row
-    pay[34:35, 0:ORDER] = jnp.sum(proj * weights[...], axis=0, keepdims=True)
-
+    grad_first_rows = jnp.concatenate(
+        [
+            (p_cos * cos_at - p_sin * sin_at) * freq_row,
+            (p_cos * sin_at + p_sin * cos_at) * freq_row,
+        ],
+        axis=0,
+    )
+    spare[...] = jnp.zeros((8, LANES), f32)
+    spare[0:1, 0:ORDER] = (p_lin + start_frac * p_one) * freq_row
+    spare[1:2, 0:ORDER] = p_one * freq_row
+    spare[2:3, 0:ORDER] = jnp.sum(proj * weights[...], axis=0, keepdims=True)
+    moved = pltpu.roll(spare[...], ORDER, 1)
+    for at in range(PLANE):
+        pay[at, :, 0:ORDER] = grad_first_rows[at : at + 1, :]
+        pay[at, :, ORDER:LANES] = (
+            moved[at : at + 1, ORDER:LANES] if at < 3 else jnp.zeros((1, ORDER), f32)
+        )
+
+    def send_each(source, target, slot, at, place, own, count, fixed):
+        def body(step, carry):
+            peer = lax.rem(own + step, count)
+            pltpu.make_async_remote_copy(
+                src_ref=source if fixed else source.at[peer],
+                dst_ref=target.at[slot],
+                send_sem=send_sem.at[at],
+                recv_sem=recv_sem.at[at],
+                device_id=place(peer),
+                device_id_type=MESH,
+            ).start()
+            return carry
+
+        lax.fori_loop(1, count, body, 0)
+        pltpu.make_async_copy(
+            source if fixed else source.at[own], target.at[slot], recv_sem.at[at]
+        ).start()
+
+    def in_ctx(at):
+        return {"ctx": at}
+
+    above = (Y_ALL - 1 - yy) * FLAT + (Z_HI - 1 - zh) * Z_LO
+
+    @pl.when(above > 0)
+    def _():
+        pl.semaphore_wait(entered, above)
+
+    send_each(pay, recv_p, at_plane, 4, in_plane, at_plane, PLANE, False)
     for at in range(CTX):
-        send_p[at] = pay[at * PIECE : (at + 1) * PIECE, :]
-    send_all(send_p, recv_p, 4)
+        pay_own[at] = jnp.where(
+            lax.broadcasted_iota(jnp.int32, (1, LANES), 1) < ORDER,
+            second_part[at : at + 1, :],
+            jnp.broadcast_to(skip_sum[at : at + 1, :], (1, LANES)),
+        )
+    send_each(pay_own, recv_own, me, 7, in_ctx, me, CTX, False)
+    send_all(send_f, recv_f, 1)
+
+    def add_up(ref, count):
+        total = ref[0]
+        for at in range(1, count):
+            total = total + ref[at]
+        return total
+
+    wait_all(recv_p, 4)
+    piece[...] = add_up(recv_p, PLANE)
+    send_each(piece, recv_s, depth, 5, in_column, depth, Z_ALL, True)
+    wait_all(recv_own, 7)
+    done_own[...] = add_up(recv_own, CTX)
+    send_each(done_own, all_own, me, 8, in_ctx, me, CTX, True)
 
     wait_all(recv_f, 1)
     for at in range(N_ONE // chunk):
@@ -458,49 +537,11 @@
     send_mb[:, 1] = direct[:, LANES:].astype(bf16).reshape(CTX, ROWS, LANES)
 
 
-    wait_all(recv_p, 4)
-    own = recv_p[0]
-    for at in range(1, CTX):
-        own = own + recv_p[at]
-    piece[...] = own
-
-    def send_slab(step, carry):
-        peer = lax.rem(slab + step, SLAB)
-        pltpu.make_async_remote_copy(
-            src_ref=piece,
-            dst_ref=recv_s.at[slab],
-            send_sem=send_sem.at[5],
-            recv_sem=recv_sem.at[5],
-            device_id={"slab": peer},
-            device_id_type=MESH,
-        ).start()
-        return carry
-
-    lax.fori_loop(1, SLAB, send_slab, 0)
-    pltpu.make_async_copy(piece, recv_s.at[slab], recv_sem.at[5]).start()
     send_all(send_mb, recv_mb, 3)
 
     wait_all(recv_s, 5)
-    total = recv_s[0]
-    for at in range(1, SLAB):
-        total = total + recv_s[at]
-    summed = lax.broadcasted_iota(jnp.int32, (PIECE, LANES), 1) < ORDER
-    done[...] = jnp.where(summed, total, piece[...])
-
-    def send_done(step, carry):
-        peer = lax.rem(me + step, CTX)
-        pltpu.make_async_remote_copy(
-            src_ref=done,
-            dst_ref=recv_d.at[me],
-            send_sem=send_sem.at[6],
-            recv_sem=recv_sem.at[6],
-            device_id={"ctx": peer},
-            device_id_type=MESH,
-        ).start()
-        return carry
-
-    lax.fori_loop(1, CTX, send_done, 0)
-    pltpu.make_async_copy(done, recv_d.at[me], recv_sem.at[6]).start()
+    done[...] = add_up(recv_s, Z_ALL)
+    send_each(done, recv_d, at_plane, 6, in_plane, at_plane, PLANE, True)
 
     wait_all(recv_mb, 3)
     flat_a[...] = recv_mb[:, 0].astype(f32).reshape(N_ONE, LANES)
@@ -517,12 +558,17 @@
     wait_sent(send_f, CTX - 1, 1)
     wait_sent(send_gf, CTX - 1, 2)
     wait_sent(send_mb, CTX - 1, 3)
-    wait_sent(send_p, CTX - 1, 4)
-    wait_sent(recv_s, SLAB - 1, 5)
+    wait_sent(pay, PLANE - 1, 4)
+    wait_sent(recv_s, Z_ALL - 1, 5)
+    wait_sent(pay_own, CTX - 1, 7)
+    wait_sent(all_own, CTX - 1, 8)
+    wait_all(all_own, 8)
+    for at in range(CTX):
+        sums_out[PLANE + at : PLANE + at + 1, :] = all_own[at]
     wait_all(recv_d, 6)
-    for at in range(CTX):
-        sums_out[at * PIECE : (at + 1) * PIECE, :] = recv_d[at]
-    wait_sent(recv_d, CTX - 1, 6)
+    for at in range(PLANE):
+        sums_out[at : at + 1, :] = recv_d[at]
+    wait_sent(recv_d, PLANE - 1, 6)
 
 
 def last_kernel(
@@ -548,11 +594,14 @@
     ]
     for store in stores:
         store.start()
-    first_out[...] = sums_ref[0:33, 0:ORDER]
-    bias_out[...] = sums_ref[33:34, 0:ORDER].reshape(ORDER)
-    freq_out[...] = sums_ref[34:35, 0:ORDER].reshape(ORDER)
-    second_out[...] = sums_ref[0:CHAN, ORDER : 2 * ORDER]
-    skip_out[...] = sums_ref[CHAN : CHAN + 1, ORDER : ORDER + CHAN].reshape(CHAN)
+    first_out[1 : 1 + 2 * BANDS, :] = sums_ref[0 : 2 * BANDS, 0:ORDER]
+    upper = pltpu.roll(sums_ref[0:8, :], ORDER, 1)
+    first_out[0:1, :] = upper[0:1, 0:ORDER]
+    bias_out[...] = upper[1:2, 0:ORDER].reshape(ORDER)
+    freq_out[...] = upper[2:3, 0:ORDER].reshape(ORDER)
+    second_out[...] = sums_ref[PLANE : PLANE + CHAN, 0:ORDER]
+    skip_row = as_row(sums_ref[PLANE : PLANE + CHAN, ORDER : ORDER + 1], CHAN)
+    skip_out[...] = skip_row.reshape(CHAN)
     for store in stores:
         store.wait()
 
@@ -577,7 +626,7 @@
     blocks = (CTX, ROWS, LANES)
     pairs = (CTX, 2, ROWS, LANES)
     rows = jax.ShapeDtypeStruct((CHAN, PART), bf16)
-    sums_shape = jax.ShapeDtypeStruct((CTX * PIECE, LANES), f32)
+    sums_shape = jax.ShapeDtypeStruct((PLANE + CTX, LANES), f32)
     query_g, key_g, value_g, sums = pl.pallas_call(
         main_kernel,
         name="hyena_backward",
@@ -626,16 +675,21 @@
             block(2 * N_ONE, 2 * LANES),
             block(3 * CHAN, PART),
             block(2 * ORDER, PART),
-            wide(CTX * PIECE, LANES),
-            wide(CTX, PIECE, LANES),
-            wide(CTX, PIECE, LANES),
-            wide(PIECE, LANES),
-            wide(SLAB, PIECE, LANES),
-            wide(PIECE, LANES),
-            wide(CTX, PIECE, LANES),
+            wide(8, LANES),
+            wide(PLANE, 1, LANES),
+            wide(PLANE, 1, LANES),
+            wide(1, LANES),
+            wide(Z_ALL, 1, LANES),
+            wide(1, LANES),
+            wide(PLANE, 1, LANES),
+            wide(CTX, 1, LANES),
+            wide(CTX, 1, LANES),
+            wide(1, LANES),
+            wide(CTX, 1, LANES),
             pltpu.SemaphoreType.DMA((18,)),
-            pltpu.SemaphoreType.DMA((7,)),
-            pltpu.SemaphoreType.DMA((7,)),
+            pltpu.SemaphoreType.DMA((9,)),
+            pltpu.SemaphoreType.DMA((9,)),
+            pltpu.SemaphoreType.REGULAR,
         ],
         compiler_params=pltpu.CompilerParams(
             collective_id=0, has_side_effects=True, vmem_limit_bytes=40 * 1024 * 1024

time: 55 us -> 51 us (0.927)
  Pallas kernels: 54.2 us -> 50.2 us
    pallas_call x1, Pallas kernels: 52.8 us -> 48.8 us  [shards(): pl.pallas_call(main_kernel, name='hyena_backward', out_shape=(rows, rows,...]
where the time goes in v3:
time: 51 us; the launch traced here: 50.9 us
  Pallas kernels  50.2 us (98%)
  between operations  0.64 us (1%)
    pallas_call x1, Pallas kernels, shards(): pl.pallas_call(main_kernel, name='hyena_backward', out_shape=(rows, rows,...  48.8 us
    pallas_call x1, Pallas kernels, shards(): pl.pallas_call(last_kernel, name='results', out_shape=(rows, rows, rows,...  1.39 us

profile of v3, /device:TPU:1, one launch (start us, length us, event | category | flops | bytes accessed | tf_op | source)
XLA Modules:
  0.0 50.9 jit_solution(2440519959487916223)
XLA Ops:
  0.6 48.8 %hyena_backward.1 = (bf16[32,2048]{1,0:T(8,128)(2,1)S(1)}, bf16[32,2048]{1,0:T(8,128)(2,1)S(1)}, bf16[32,2048]{1,0:T(8,128)(2,1)S(1)}, f32[64,128]{1,0:T(8,128)S(1)}) custom-call(bf16[32,2048]{1,0:T(8,128)(2,1)} %query_hbm.1, bf16[32,2048]{1,0:T(8,128)(2,1)} %key_hbm.1, bf16[32,2048]{1,0:T(8,128)(2,1)} %value_hbm.1, bf16[32,2048]{1,0:T(8,128)(2,1)} %grad_hbm.1, ...), custom_call_target="tpu_custom_call" | custom-call | tf_op jit(solution)/shard_map/hyena_backward/pallas_call | solution.py:630
  49.5 1.4 %results.1 = (bf16[32,2048]{1,0:T(8,128)(2,1)}, bf16[32,2048]{1,0:T(8,128)(2,1)}, bf16[32,2048]{1,0:T(8,128)(2,1)}, f32[33,64]{1,0:T(8,128)}, f32[64]{0:T(128)},...) custom-call(bf16[32,2048]{1,0:T(8,128)(2,1)S(1)} %get-tuple-element.20.query_ref, ...), custom_call_target="tpu_custom_call" | custom-call | tf_op jit(solution)/shard_map/results/pallas_call | solution.py:713

commit v4 on v3

--- a/solution.py
+++ b/solution.py
@@ -242,7 +242,8 @@
 
         lax.fori_loop(first_at, last_at, body, 0)
 
-    lax.fori_loop(1, CTX, greet_ctx, 0)
+    lax.fori_loop(FLAT, CTX, greet_ctx, 0)
+    lax.fori_loop(1, FLAT, greet_ctx, 0)
     signal_each(barrier, in_plane, (yy + 1) * FLAT, PLANE)
     signal_each(barrier, in_column, (zh + 1) * Z_LO, Z_ALL)
 
@@ -415,8 +416,27 @@
         d_real, d_imag = inverse_part(w_r * g_r + w_i * g_i, w_r * g_i - w_i * g_r, cos_t, sin_t)
         fold_a[rows, :] = d_real
         fold_a[low_rows, :] = d_imag
-    send_gf[...] = dot(first_t[...], fold_a[...]).astype(bf16).reshape(CTX, ROWS, LANES)
-    send_all(send_gf, recv_gf, 2)
+    group = CTX // 4
+    for at in range(4):
+        part = dot(first_t[at * N_ONE // 4 : (at + 1) * N_ONE // 4, :], fold_a[...])
+        send_gf[at * group : (at + 1) * group] = part.astype(bf16).reshape(group, ROWS, LANES)
+
+        def send_part(peer, carry):
+            @pl.when(peer != me)
+            def _():
+                pltpu.make_async_remote_copy(
+                    src_ref=send_gf.at[peer],
+                    dst_ref=recv_gf.at[me],
+                    send_sem=send_sem.at[2],
+                    recv_sem=recv_sem.at[2],
+                    device_id={"ctx": peer},
+                    device_id_type=MESH,
+                ).start()
+
+            return carry
+
+        lax.fori_loop(at * group, (at + 1) * group, send_part, 0)
+    pltpu.make_async_copy(send_gf.at[me], recv_gf.at[me], recv_sem.at[2]).start()
 
     wait_all(recv_gf, 2)
     flat_a[...] = recv_gf[...].astype(f32).reshape(N_ONE, LANES)
@@ -431,13 +451,6 @@
     high, low = high_low(grad_hidden * cosines[...])
     grad_sin[0:ORDER, :] = high
     grad_sin[ORDER : 2 * ORDER, :] = low
-    second_part = dot_last(grad_mod[0 : 2 * CHAN, :], hidden[...])
-    high_part = second_part[:CHAN]
-    low_part = jnp.where(
-        lax.broadcasted_iota(jnp.int32, (CHAN, LANES), 1) < ORDER, second_part[CHAN:], 0.0
-    )
-    second_part = high_part + low_part
-    second_part = second_part + pltpu.roll(second_part, ORDER, 1)
     proj = dot_last(pair[...], grad_sin[0:ORDER, :])
     proj = proj[0:KROWS] + proj[48 : 48 + KROWS] + dot_last(pair[0:48, :], grad_sin[ORDER:, :])[0:KROWS]
     p_cos, p_sin = proj[0:BANDS], proj[BANDS : 2 * BANDS]
@@ -488,6 +501,13 @@
         pl.semaphore_wait(entered, above)
 
     send_each(pay, recv_p, at_plane, 4, in_plane, at_plane, PLANE, False)
+    second_part = dot_last(grad_mod[0 : 2 * CHAN, :], hidden[...])
+    high_part = second_part[:CHAN]
+    low_part = jnp.where(
+        lax.broadcasted_iota(jnp.int32, (CHAN, LANES), 1) < ORDER, second_part[CHAN:], 0.0
+    )
+    second_part = high_part + low_part
+    second_part = second_part + pltpu.roll(second_part, ORDER, 1)
     for at in range(CTX):
         pay_own[at] = jnp.where(
             lax.broadcasted_iota(jnp.int32, (1, LANES), 1) < ORDER,
@@ -584,26 +604,38 @@
     freq_out,
     second_out,
     skip_out,
+    first_ref,
+    bias_ref,
+    freq_ref,
+    second_ref,
+    skip_ref,
     sem,
 ):
-    stores = [
-        pltpu.make_async_copy(source, target, sem.at[at])
-        for at, (source, target) in enumerate(
-            [(query_ref, query_out), (key_ref, key_out), (value_ref, value_out)]
-        )
-    ]
-    for store in stores:
-        store.start()
-    first_out[1 : 1 + 2 * BANDS, :] = sums_ref[0 : 2 * BANDS, 0:ORDER]
+    stores = []
+
+    def store(source, target):
+        copy = pltpu.make_async_copy(source, target, sem.at[len(stores)])
+        copy.start()
+        stores.append(copy)
+
+    store(query_ref, query_out)
+    store(key_ref, key_out)
+    store(value_ref, value_out)
+    first_ref[1 : 1 + 2 * BANDS, :] = sums_ref[0 : 2 * BANDS, 0:ORDER]
     upper = pltpu.roll(sums_ref[0:8, :], ORDER, 1)
-    first_out[0:1, :] = upper[0:1, 0:ORDER]
-    bias_out[...] = upper[1:2, 0:ORDER].reshape(ORDER)
-    freq_out[...] = upper[2:3, 0:ORDER].reshape(ORDER)
-    second_out[...] = sums_ref[PLANE : PLANE + CHAN, 0:ORDER]
+    first_ref[0:1, :] = upper[0:1, 0:ORDER]
+    store(first_ref, first_out)
+    bias_ref[...] = upper[1:2, 0:ORDER].reshape(ORDER)
+    store(bias_ref, bias_out)
+    freq_ref[...] = upper[2:3, 0:ORDER].reshape(ORDER)
+    store(freq_ref, freq_out)
+    second_ref[...] = sums_ref[PLANE : PLANE + CHAN, 0:ORDER]
+    store(second_ref, second_out)
     skip_row = as_row(sums_ref[PLANE : PLANE + CHAN, ORDER : ORDER + 1], CHAN)
-    skip_out[...] = skip_row.reshape(CHAN)
-    for store in stores:
-        store.wait()
+    skip_ref[...] = skip_row.reshape(CHAN)
+    store(skip_ref, skip_out)
+    for copy in stores:
+        copy.wait()
 
 
 def shards(
@@ -724,8 +756,15 @@
             vector(CHAN),
         ),
         in_specs=[vmem] * 4,
-        out_specs=(hbm, hbm, hbm, vmem, vmem, vmem, vmem, vmem),
-        scratch_shapes=[pltpu.SemaphoreType.DMA((3,))],
+        out_specs=tuple([hbm] * 8),
+        scratch_shapes=[
+            wide(33, ORDER),
+            wide(ORDER),
+            wide(ORDER),
+            wide(CHAN, ORDER),
+            wide(CHAN),
+            pltpu.SemaphoreType.DMA((8,)),
+        ],
         compiler_params=pltpu.CompilerParams(vmem_limit_bytes=56 * 1024 * 1024),
     )(*[pltpu.with_memory_space_constraint(held, pltpu.VMEM) for held in (query_g, key_g, value_g, sums)])
     return (*outs[:6], outs[6].T, outs[7])

time: 51 us -> 49.8 us (0.976)
  Pallas kernels: 50.2 us -> 49.1 us
    pallas_call x1, Pallas kernels: 48.8 us -> 48.2 us  [shards(): pl.pallas_call(main_kernel, name='hyena_backward', out_shape=(rows, rows,...]
    pallas_call x1, Pallas kernels: 1.39 us -> 0.82 us  [shards(): pl.pallas_call(last_kernel, name='results', out_shape=(rows, rows, rows,...]
where the time goes in v4:
time: 49.8 us; the launch traced here: 49.7 us
  Pallas kernels  49.1 us (99%)
  between operations  0.64 us (1%)
    pallas_call x1, Pallas kernels, shards(): pl.pallas_call(main_kernel, name='hyena_backward', out_shape=(rows, rows,...  48.2 us

profile of v4, /device:TPU:1, one launch (start us, length us, event | category | flops | bytes accessed | tf_op | source)
XLA Modules:
  0.0 49.7 jit_solution(14914265030470982975)
XLA Ops:
  0.6 48.2 %hyena_backward.1 = (bf16[32,2048]{1,0:T(8,128)(2,1)S(1)}, bf16[32,2048]{1,0:T(8,128)(2,1)S(1)}, bf16[32,2048]{1,0:T(8,128)(2,1)S(1)}, f32[64,128]{1,0:T(8,128)S(1)}) custom-call(bf16[32,2048]{1,0:T(8,128)(2,1)} %query_hbm.1, bf16[32,2048]{1,0:T(8,128)(2,1)} %key_hbm.1, bf16[32,2048]{1,0:T(8,128)(2,1)} %value_hbm.1, bf16[32,2048]{1,0:T(8,128)(2,1)} %grad_hbm.1, ...), custom_call_target="tpu_custom_call" | custom-call | tf_op jit(solution)/shard_map/hyena_backward/pallas_call | solution.py:662
  48.9 0.8 %results.1 = (bf16[32,2048]{1,0:T(8,128)(2,1)}, bf16[32,2048]{1,0:T(8,128)(2,1)}, bf16[32,2048]{1,0:T(8,128)(2,1)}, f32[33,64]{1,0:T(8,128)}, f32[64]{0:T(128)},...) custom-call(bf16[32,2048]{1,0:T(8,128)(2,1)S(1)} %get-tuple-element.20.query_ref, ...), custom_call_target="tpu_custom_call" | custom-call | tf_op jit(solution)/shard_map/results/pallas_call | solution.py:745

commit v5 on v4

--- a/solution.py
+++ b/solution.py
@@ -185,6 +185,7 @@
     cosines,
     modul,
     both,
+    partial,
     spec_w,
     spec_g,
     fold_a,
@@ -291,21 +292,23 @@
         for copy in copies:
             copy.wait()
 
-    def send_all(source, target, at):
+    def send_all(source, target, at, arrival=None):
+        arrival = at if arrival is None else arrival
+
         def body(step, carry):
             peer = lax.rem(me + step, CTX)
             pltpu.make_async_remote_copy(
                 src_ref=source.at[peer],
                 dst_ref=target.at[me],
                 send_sem=send_sem.at[at],
-                recv_sem=recv_sem.at[at],
+                recv_sem=recv_sem.at[arrival],
                 device_id={"ctx": peer},
                 device_id_type=MESH,
             ).start()
             return carry
 
         lax.fori_loop(1, CTX, body, 0)
-        pltpu.make_async_copy(source.at[me], target.at[me], recv_sem.at[at]).start()
+        pltpu.make_async_copy(source.at[me], target.at[me], recv_sem.at[arrival]).start()
 
     def wait_all(target, at):
         pltpu.make_async_copy(target, target, recv_sem.at[at]).wait()
@@ -376,14 +379,23 @@
     send_f[...] = flat_a[...].reshape(CHAN, ROWS, LANES).astype(bf16)
 
     pl.semaphore_wait(barrier, CTX - 1 + yy * FLAT + zh * Z_LO)
-    send_all(send_mg, recv_mg, 0)
+    send_all(send_mg, recv_mg, 0, 9 + zl)
     signal_each(entered, in_plane, 0, yy * FLAT)
     signal_each(entered, in_column, 0, zh * Z_LO)
 
     wait_loads(transforms)
-    wait_all(recv_mg, 0)
-    both[:, 0:LANES] = recv_mg[:, 0].reshape(N_ONE, LANES)
-    both[:, LANES : 2 * LANES] = recv_mg[:, 1].reshape(N_ONE, LANES)
+    for at in range(Z_LO):
+        group = lax.rem(zl + Z_LO - at, Z_LO)
+        sources = pl.ds(group * FLAT, FLAT)
+        arrived = recv_mg.at[sources]
+        pltpu.make_async_copy(arrived, arrived, recv_sem.at[9 + group]).wait()
+        inner = pl.ds(pl.multiple_of(group * LANES, LANES), LANES)
+        both[inner, 0:LANES] = recv_mg[sources, 0].reshape(LANES, LANES)
+        both[inner, LANES : 2 * LANES] = recv_mg[sources, 1].reshape(LANES, LANES)
+        if at == 0:
+            partial[...] = dot(first[:, inner], both[inner, :])
+        elif at < Z_LO - 1:
+            partial[...] += dot(first[:, inner], both[inner, :])
     chunk = 256
 
     def turned(rows):
@@ -406,8 +418,8 @@
         rows = pl.ds(at * chunk, chunk)
         low_rows = pl.ds(N_ONE + at * chunk, chunk)
         cos_t, sin_t = turned(rows)
-        a_real = dot(first[rows, :], both[...])
-        a_imag = dot(first[low_rows, :], both[...])
+        a_real = partial[rows, :] + dot(first[rows, inner], both[inner, :])
+        a_imag = partial[low_rows, :] + dot(first[low_rows, inner], both[inner, :])
         w_spec = spectrum(a_real[:, :LANES], a_imag[:, :LANES], cos_t, sin_t)
         g_spec = spectrum(a_real[:, LANES:], a_imag[:, LANES:], cos_t, sin_t)
         spec_w[rows, :] = w_spec
@@ -701,6 +713,7 @@
             wide(ORDER, PART),
             wide(CHAN, PART),
             block(N_ONE, 2 * LANES),
+            wide(2 * N_ONE, 2 * LANES),
             wide(N_ONE, 2 * LANES),
             wide(N_ONE, 2 * LANES),
             block(2 * N_ONE, LANES),
@@ -720,7 +733,7 @@
             wide(CTX, 1, LANES),
             pltpu.SemaphoreType.DMA((18,)),
             pltpu.SemaphoreType.DMA((9,)),
-            pltpu.SemaphoreType.DMA((9,)),
+            pltpu.SemaphoreType.DMA((13,)),
             pltpu.SemaphoreType.REGULAR,
         ],
         compiler_params=pltpu.CompilerParams(

time: 49.8 us -> 50.1 us (level)
  no operation moved by 1% of the time
where the time goes in v5:
time: 50.1 us; the launch traced here: 50 us
  Pallas kernels  49.3 us (98%)
  between operations  0.64 us (1%)
    pallas_call x1, Pallas kernels, shards(): pl.pallas_call(main_kernel, name='hyena_backward', out_shape=(rows, rows,...  48.5 us

profile of v5, /device:TPU:1, one launch (start us, length us, event | category | flops | bytes accessed | tf_op | source)
XLA Modules:
  0.0 50.0 jit_solution(5466010410224420485)
XLA Ops:
  0.6 48.5 %hyena_backward.1 = (bf16[32,2048]{1,0:T(8,128)(2,1)S(1)}, bf16[32,2048]{1,0:T(8,128)(2,1)S(1)}, bf16[32,2048]{1,0:T(8,128)(2,1)S(1)}, f32[64,128]{1,0:T(8,128)S(1)}) custom-call(bf16[32,2048]{1,0:T(8,128)(2,1)} %query_hbm.1, bf16[32,2048]{1,0:T(8,128)(2,1)} %key_hbm.1, bf16[32,2048]{1,0:T(8,128)(2,1)} %value_hbm.1, bf16[32,2048]{1,0:T(8,128)(2,1)} %grad_hbm.1, ...), custom_call_target="tpu_custom_call" | custom-call | tf_op jit(solution)/shard_map/hyena_backward/pallas_call | solution.py:674
  49.1 0.8 %results.1 = (bf16[32,2048]{1,0:T(8,128)(2,1)}, bf16[32,2048]{1,0:T(8,128)(2,1)}, bf16[32,2048]{1,0:T(8,128)(2,1)}, f32[33,64]{1,0:T(8,128)}, f32[64]{0:T(128)},...) custom-call(bf16[32,2048]{1,0:T(8,128)(2,1)S(1)} %get-tuple-element.20.query_ref, ...), custom_call_target="tpu_custom_call" | custom-call | tf_op jit(solution)/shard_map/results/pallas_call | solution.py:758
